TPU v7x, 256 devices: a whole 4x4x8 slice. The times are simulated.
256 devices in a mesh: dom: 64 (over x, y_hi, z), col: 4 (over y_lo, core).
Axes of the slice: x: 4, y: 4 (y_hi: 2, y_lo: 2; y = y_hi * 2 + y_lo), z: 8, core: 2. Of those that a mesh axis runs over, the one named last changes fastest.
Arguments:
- l_values: bfloat16 [2304, 64, 448], P(('dom', 'col')), may hold values from -0.375 to 0.375
- s_values: bfloat16 [2304, 64, 448], P(('dom', 'col')), may hold values from -6 to 6
- h_values: bfloat16 [2304, 64, 448], P(('dom', 'col')), may hold values from -0.375 to 0.375
- pattern: int32 [2304, 7], replicated, may hold values 0 or 1
Outputs:
- kernel: bfloat16 [2304, 64, 448], P(('dom', 'col'))
- gradient: bfloat16 [2304, 64, 448], P(('dom', 'col'))
All inputs are finite; a program needn't handle non-finite values.
Results may differ from a plain program's by a relative error of at most 0.0064.
Values may be sent and summed in bfloat16 or wider, within the bound.
No kernel may reach another device: no remote copies, remote signals or barrier semaphores. Data moves between devices by JAX's collectives and lax.ppermute only.
A program may use at most 128 MiB of HBM per device.

v0:
```python
import jax
import jax.numpy as jnp
from jax import lax
from jax.sharding import PartitionSpec as P


def padded_2(cells, sides, width):
    for axis, dim in sides:
        count = lax.axis_size(axis)
        head = lax.slice_in_dim(cells, 0, width, axis=dim)
        tail = lax.slice_in_dim(cells, cells.shape[dim] - width, cells.shape[dim], axis=dim)
        cells = jnp.concatenate(
            [
                lax.ppermute(tail, axis, [(i, (i + 1) % count) for i in range(count)]),
                cells,
                lax.ppermute(head, axis, [((i + 1) % count, i) for i in range(count)]),
            ],
            axis=dim,
        )
    return cells


def truncated(left_matrix, right_near, pattern_rows):
    row_count, block_size, row_width = left_matrix.shape
    slot_count = row_width // block_size
    reach_len = (slot_count - 1) // 2
    padded = jnp.pad(right_near, ((0, 0), (0, 0), (reach_len * block_size, reach_len * block_size)))
    slabs = []
    for inner in range(slot_count):
        start = (2 * reach_len - inner) * block_size
        slabs.append(padded[inner : inner + row_count, :, start : start + row_width])
    panels = jnp.stack(slabs, axis=1).reshape(row_count, slot_count * block_size, row_width)
    accumulated = jnp.einsum(
        "irk,ikn->irn", left_matrix, panels, preferred_element_type=jnp.float32
    )
    accumulated = accumulated.reshape(row_count, block_size, slot_count, block_size)
    keep_mask = pattern_rows.astype(jnp.float32)[:, None, :, None]
    return (accumulated * keep_mask).reshape(row_count, block_size, row_width)


def masked(values, pattern_rows):
    row_count, block_size, row_width = values.shape
    slot_count = row_width // block_size
    four = values.reshape(row_count, block_size, slot_count, block_size)
    return (four * pattern_rows.astype(jnp.bfloat16)[:, None, :, None]).reshape(values.shape)


def shards(l_values, s_values, h_values, pattern):
    row_count, block_size, row_width = l_values.shape
    slot_count = row_width // block_size
    reach_len = (slot_count - 1) // 2
    total_rows = pattern.shape[0]
    first_row = lax.axis_index(("dom", "col")) * row_count
    indices = (first_row - 0 + jnp.arange(row_count + 2 * 0, dtype=jnp.int32)) % total_rows
    local_pattern = jnp.take(pattern, indices, axis=0)
    l_masked = masked(l_values, local_pattern)
    s_masked = masked(s_values, local_pattern)
    h_masked = masked(h_values, local_pattern)
    s_near, l_near = (
        padded_2(s_masked, ((("dom", "col"), 0),), reach_len),
        padded_2(l_masked, ((("dom", "col"), 0),), reach_len),
    )
    product_ls = truncated(l_masked, s_near, local_pattern).astype(jnp.bfloat16)
    product_near = padded_2(product_ls, ((("dom", "col"), 0),), reach_len)
    hls_term = truncated(h_masked, product_near, local_pattern).astype(jnp.bfloat16)
    hls_near = padded_2(hls_term, ((("dom", "col"), 0),), reach_len)
    lsl_term = truncated(product_ls, l_near, local_pattern).astype(jnp.bfloat16)
    quintic = truncated(lsl_term, product_near, local_pattern)
    kernel = (3.0 * lsl_term.astype(jnp.float32) - 2.0 * quintic).astype(jnp.bfloat16)
    hls_four = hls_near.reshape(row_count + 2 * reach_len, block_size, slot_count, block_size)
    pieces = []
    for offset in range(slot_count):
        source = hls_four[offset : offset + row_count, :, 2 * reach_len - offset, :]
        pieces.append(jnp.transpose(source, (0, 2, 1)))
    mirrored = jnp.stack(pieces, axis=2)
    keep_mask = local_pattern.astype(jnp.float32)[:, None, :, None]
    summed = hls_term.reshape(row_count, block_size, slot_count, block_size).astype(
        jnp.float32
    ) + mirrored.astype(jnp.float32)
    gradient = (summed * keep_mask).reshape(row_count, block_size, row_width).astype(jnp.bfloat16)
    return (kernel, gradient)


def solution(mesh):
    return jax.shard_map(
        shards,
        mesh=mesh,
        in_specs=(
            P(("dom", "col"), None, None),
            P(("dom", "col"), None, None),
            P(("dom", "col"), None, None),
            P(),
        ),
        out_specs=(P(("dom", "col"), None, None), P(("dom", "col"), None, None)),
        check_vma=False,
    )
```

profile of v0, /device:TPU:0, one launch (start us, length us, event | category | flops | bytes accessed | tf_op | source)
XLA Modules:
  0.0 86.3 jit_solution(12991578538908959750)
XLA Ops:
  0.7 2.4 %copy.28 = s32[2304,7]{1,0:T(8,128)} copy(s32[2304,7]{0,1:T(8,128)} %param.7) | data formatting | bytes 129024 | tf_op args[3]
  3.1 1.8 %reshape.124 = bf16[9,64,7,64]{3,2,1,0:T(8,128)(2,1)S(1)} reshape(bf16[9,64,448]{2,1,0:T(8,128)(2,1)} %param.4) | data formatting | bytes 1032192 | tf_op jit(solution)/shard_map/reshape | solution.py:44
  4.9 0.7 reshape.122
  5.6 1.8 %gather_fusion = s32[9,7]{1,0:T(8,128)S(1)} fusion(s32[2304,7]{1,0:T(8,128)} %copy.28, s32[1024]{0:T(1024)S(1)} %pad_clamp_fusion), kind=kCustom, calls=%fused_computation | custom fusion | bytes 540 | tf_op jit(solution)/shard_map/jit(_take)/gather | solution.py:55
  7.8 0.3 slice.137
  8.0 8.3 %collective-permute-start.3 = (bf16[3,64,448]{2,1,0:T(8,128)(2,1)S(1)}, bf16[3,64,448]{2,1,0:T(8,128)(2,1)}, u32[]{:S(2)}, u32[]{:S(2)}) collective-permute-start(bf16[3,64,448]{2,1,0:T(8,128)(2,1)S(1)} %slice.137), channel_id=1, source_target_pairs={{1,0},{2,1},{3,2},{4,3},{5,4},{6,5},{7,6},{8,7},{9,8},{10,9},{11,1... | collective-permute-start | bytes 516104 | tf_op jit(solution)/shard_map/ppermute | solution.py:16
  16.7 0.3 slice.127
  17.0 7.2 %collective-permute-start.1 = (bf16[3,64,448]{2,1,0:T(8,128)(2,1)S(1)}, bf16[3,64,448]{2,1,0:T(8,128)(2,1)S(1)}, u32[]{:S(2)}, u32[]{:S(2)}) collective-permute-start(bf16[3,64,448]{2,1,0:T(8,128)(2,1)S(1)} %slice.127), channel_id=1, source_target_pairs={{1,0},{2,1},{3,2},{4,3},{5,4},{6,5},{7,6},{8,7},{9,8},{10,9},{11,1... | collective-permute-start | bytes 516104 | tf_op jit(solution)/shard_map/ppermute | solution.py:16
  25.0 2.3 %collective-permute-done.2 = bf16[3,64,448]{2,1,0:T(8,128)(2,1)} collective-permute-done((bf16[3,64,448]{2,1,0:T(8,128)(2,1)S(1)}, bf16[3,64,448]{2,1,0:T(8,128)(2,1)}, u32[]{:S(2)}, u32[]{:S(2)}) %collective-permute-start.2) | collective-permute-done | bytes 172064 | tf_op jit(solution)/shard_map/ppermute | solution.py:14
  27.4 7.7 %collective-permute-done = bf16[3,64,448]{2,1,0:T(8,128)(2,1)S(1)} collective-permute-done((bf16[3,64,448]{2,1,0:T(8,128)(2,1)S(1)}, bf16[3,64,448]{2,1,0:T(8,128)(2,1)S(1)}, u32[]{:S(2)}, u32[]{:S(2)}) %collective-permute-start) | collective-permute-done | bytes 172064 | tf_op jit(solution)/shard_map/ppermute | solution.py:14
  35.1 2.4 %select_maximum_fusion.2 = (bf16[15,64,832]{2,1,0:T(8,128)(2,1)S(1)}, bf16[15,64,832]{2,1,0:T(8,128)(2,1)S(1)}) fusion(bf16[3,64,448]{2,1,0:T(8,128)(2,1)} %collective-permute-done.3, bf16[9,64,448]{2,1,0:T(8,128)(2,1)S(1)} %get-tuple-element.18, bf16[3,64,448]{2,1,0:T(8,128)(2,1)} %collective-permute-done.2, ...), kind=kLoop, calls=%fused_computation.6 | loop fusion | flops 16773120 | bytes 4915200 | tf_op jit(solution)/shard_map/concatenate | solution.py:12
  37.6 0.3 fusion.23
  38.1 0.3 fusion.20
  38.4 0.5 copy.29
  39.0 0.3 fusion.17
  39.5 0.3 fusion.14
  39.9 0.5 copy.30
  40.4 0.8 fusion.3
  41.3 0.5 collective-permute-start.4
  41.8 0.8 fusion.4
  42.7 1.8 %collective-permute-done.5 = bf16[3,64,448]{2,1,0:T(8,128)(2,1)S(1)} collective-permute-done((bf16[3,64,448]{2,1,0:T(8,128)(2,1)S(1)}, bf16[3,64,448]{2,1,0:T(8,128)(2,1)S(1)}, u32[]{:S(2)}, u32[]{:S(2)}) %collective-permute-start.5) | collective-permute-done | bytes 172064 | tf_op jit(solution)/shard_map/ppermute | solution.py:16
  44.5 7.6 %collective-permute-done.4 = bf16[3,64,448]{2,1,0:T(8,128)(2,1)S(1)} collective-permute-done((bf16[3,64,448]{2,1,0:T(8,128)(2,1)S(1)}, bf16[3,64,448]{2,1,0:T(8,128)(2,1)S(1)}, u32[]{:S(2)}, u32[]{:S(2)}) %collective-permute-start.4) | collective-permute-done | bytes 172064 | tf_op jit(solution)/shard_map/ppermute | solution.py:14
  52.1 0.5 select_maximum_fusion
  52.7 0.3 fusion.11
  53.2 0.3 fusion.8
  53.6 0.5 copy.31
  54.1 0.6 copy-done.5
  54.7 0.8 fusion.6
  55.7 0.5 collective-permute-start.6
  56.2 1.6 %fusion.5 = bf16[9,64,448]{2,1,0:T(8,128)(2,1)} fusion(bf16[9,64,448]{2,1,0:T(8,128)(2,1)S(1)} %fusion.4, bf16[9,448,448]{2,1,0:T(8,128)(2,1)S(1)} %bitcast.140, f32[9,448]{1,0:T(8,128)S(1)} %mul.102), kind=kOutput, calls=%fused_computation.18 | convolution fusion | flops 232759296 | bytes 4660992 | tf_op jit(solution)/shard_map/irk,ikn->irn/dot_general | solution.py:33
  57.8 1.0 %collective-permute-done.7 = bf16[3,64,448]{2,1,0:T(8,128)(2,1)S(1)} collective-permute-done((bf16[3,64,448]{2,1,0:T(8,128)(2,1)S(1)}, bf16[3,64,448]{2,1,0:T(8,128)(2,1)S(1)}, u32[]{:S(2)}, u32[]{:S(2)}) %collective-permute-start.7) | collective-permute-done | bytes 172064 | tf_op jit(solution)/shard_map/ppermute | solution.py:16
  58.8 7.4 %collective-permute-done.6 = bf16[3,64,448]{2,1,0:T(8,128)(2,1)S(1)} collective-permute-done((bf16[3,64,448]{2,1,0:T(8,128)(2,1)S(1)}, bf16[3,64,448]{2,1,0:T(8,128)(2,1)S(1)}, u32[]{:S(2)}, u32[]{:S(2)}) %collective-permute-start.6) | collective-permute-done | bytes 172064 | tf_op jit(solution)/shard_map/ppermute | solution.py:14
  66.4 1.2 %reshape.127 = bf16[15,64,7,64]{3,2,1,0:T(8,128)(2,1)S(1)} reshape(bf16[15,64,448]{2,1,0:T(8,128)(2,1)S(1)} %pad_maximum_fusion) | data formatting | bytes 1720320 | tf_op jit(solution)/shard_map/reshape | solution.py:70
  67.6 3.4 %fusion.28 = (bf16[9,64,1,64]{3,2,1,0:T(2,128)(2,1)S(1)}, bf16[9,64,1,64]{3,2,1,0:T(2,128)(2,1)S(1)}, bf16[9,64,1,64]{3,2,1,0:T(2,128)(2,1)S(1)}, bf16[9,64,1,64...) fusion(bf16[15,64,7,64]{3,2,1,0:T(8,128)(2,1)S(1)} %reshape.127), kind=kLoop, calls=%fused_computation.83 | loop fusion | bytes 1032192 | tf_op jit(solution)/shard_map/slice | solution.py:73
  71.0 1.1 %copy.47 = bf16[9,64,1,64]{1,3,0,2:T(8,128)(2,1)S(1)} copy(bf16[9,64,1,64]{3,2,1,0:T(2,128)(2,1)} %get-tuple-element.8) | data formatting | bytes 147456 | tf_op jit(solution)/shard_map/transpose | solution.py:74
  72.1 0.7 bitcast_dynamic-update-slice_fusion.9
  72.8 1.1 %copy.48 = bf16[9,64,1,64]{1,3,0,2:T(8,128)(2,1)S(1)} copy(bf16[9,64,1,64]{3,2,1,0:T(2,128)(2,1)} %get-tuple-element.7) | data formatting | bytes 147456 | tf_op jit(solution)/shard_map/transpose | solution.py:74
  73.9 1.1 %copy.49 = bf16[9,64,1,64]{1,3,0,2:T(8,128)(2,1)S(1)} copy(bf16[9,64,1,64]{3,2,1,0:T(2,128)(2,1)} %get-tuple-element.6) | data formatting | bytes 147456 | tf_op jit(solution)/shard_map/transpose | solution.py:74
  75.0 1.1 %copy.50 = bf16[9,64,1,64]{1,3,0,2:T(8,128)(2,1)S(1)} copy(bf16[9,64,1,64]{3,2,1,0:T(2,128)(2,1)} %get-tuple-element.5) | data formatting | bytes 147456 | tf_op jit(solution)/shard_map/transpose | solution.py:74
  76.7 0.7 bitcast_dynamic-update-slice_fusion.8
  77.4 0.7 bitcast_dynamic-update-slice_fusion.7
  78.0 0.7 bitcast_dynamic-update-slice_fusion.6
  78.7 0.7 bitcast_dynamic-update-slice_fusion.5
  79.4 0.7 bitcast_dynamic-update-slice_fusion.4
  80.0 0.7 bitcast_dynamic-update-slice_fusion.3
  80.7 1.9 %copy.39 = f32[9,64,7,64]{3,2,1,0:T(8,128)S(1)} copy(bf16[9,64,7,64]{3,1,0,2:T(8,128)(2,1)} %bitcast_dynamic-update-slice_fusion.3) | data formatting | bytes 1548288 | tf_op jit(solution)/shard_map/convert_element_type | solution.py:79
  82.6 1.5 %reshape.128 = f32[9,64,448]{2,1,0:T(8,128)} reshape(f32[9,64,7,64]{3,2,1,0:T(8,128)S(1)} %copy.39) | data formatting | bytes 2064384 | tf_op jit(solution)/shard_map/convert_element_type | solution.py:79
  84.1 2.3 %multiply_convert_fusion = bf16[9,64,448]{2,1,0:T(8,128)(2,1)} fusion(f32[9,64,448]{2,1,0:T(8,128)} %reshape.128, bf16[9,64,448]{2,1,0:T(8,128)(2,1)S(1)} %fusion.6, f32[9,448]{1,0:T(8,128)S(1)} %copy-done.4), kind=kLoop, calls=%fused_computation.20 | loop fusion | flops 1032192 | bytes 2080512 | tf_op jit(solution)/shard_map/convert_element_type | solution.py:80
  (52 shorter events, 3.3 us)
Async XLA Ops:
  0.6 4.2 %copy-start = (bf16[9,64,448]{2,1,0:T(8,128)(2,1)S(1)}, bf16[9,64,448]{2,1,0:T(8,128)(2,1)}, u32[]{:S(2)}) copy-start(bf16[9,64,448]{2,1,0:T(8,128)(2,1)} %param.5) | copy-start | bytes 1548292
  7.7 17.2 %copy-start.1 = (bf16[9,64,448]{2,1,0:T(8,128)(2,1)S(1)}, bf16[9,64,448]{2,1,0:T(8,128)(2,1)}, u32[]{:S(2)}) copy-start(bf16[9,64,448]{2,1,0:T(8,128)(2,1)} %param.5) | copy-start | bytes 1548292
  7.7 17.2 %copy-start.2 = (bf16[9,64,448]{2,1,0:T(8,128)(2,1)S(1)}, bf16[9,64,448]{2,1,0:T(8,128)(2,1)}, u32[]{:S(2)}) copy-start(bf16[9,64,448]{2,1,0:T(8,128)(2,1)} %param.4) | copy-start | bytes 1548292
  8.0 16.9 %collective-permute-start.3 = (bf16[3,64,448]{2,1,0:T(8,128)(2,1)S(1)}, bf16[3,64,448]{2,1,0:T(8,128)(2,1)}, u32[]{:S(2)}, u32[]{:S(2)}) collective-permute-start(bf16[3,64,448]{2,1,0:T(8,128)(2,1)S(1)} %slice.137), channel_id=1, source_target_pairs={{1,0},{2,1},{3,2},{4,3},{5,4},{6,5},{7,6},{8,7},{9,8},{10,9},{11,1... | collective-permute-start | bytes 516104 | tf_op jit(solution)/shard_map/ppermute | solution.py:16
  16.6 10.7 %collective-permute-start.2 = (bf16[3,64,448]{2,1,0:T(8,128)(2,1)S(1)}, bf16[3,64,448]{2,1,0:T(8,128)(2,1)}, u32[]{:S(2)}, u32[]{:S(2)}) collective-permute-start(bf16[3,64,448]{2,1,0:T(8,128)(2,1)S(1)} %slice.135), channel_id=1, source_target_pairs={{0,1},{1,2},{2,3},{3,4},{4,5},{5,6},{6,7},{7,8},{8,9},{9,10},{10,1... | collective-permute-start | bytes 516104 | tf_op jit(solution)/shard_map/ppermute | solution.py:14
  17.0 10.4 %collective-permute-start.1 = (bf16[3,64,448]{2,1,0:T(8,128)(2,1)S(1)}, bf16[3,64,448]{2,1,0:T(8,128)(2,1)S(1)}, u32[]{:S(2)}, u32[]{:S(2)}) collective-permute-start(bf16[3,64,448]{2,1,0:T(8,128)(2,1)S(1)} %slice.127), channel_id=1, source_target_pairs={{1,0},{2,1},{3,2},{4,3},{5,4},{6,5},{7,6},{8,7},{9,8},{10,9},{11,1... | collective-permute-start | bytes 516104 | tf_op jit(solution)/shard_map/ppermute | solution.py:16
  24.5 10.6 %collective-permute-start = (bf16[3,64,448]{2,1,0:T(8,128)(2,1)S(1)}, bf16[3,64,448]{2,1,0:T(8,128)(2,1)S(1)}, u32[]{:S(2)}, u32[]{:S(2)}) collective-permute-start(bf16[3,64,448]{2,1,0:T(8,128)(2,1)S(1)} %slice.125), channel_id=1, source_target_pairs={{0,1},{1,2},{2,3},{3,4},{4,5},{5,6},{6,7},{7,8},{8,9},{9,10},{10,1... | collective-permute-start | bytes 516104 | tf_op jit(solution)/shard_map/ppermute | solution.py:14
  24.9 31.3 %copy-start.3 = (f32[9,448]{1,0:T(8,128)}, f32[9,448]{1,0:T(8,128)S(1)}, u32[]{:S(2)}) copy-start(f32[9,448]{1,0:T(8,128)S(1)} %mul.102) | copy-start | bytes 48388
  41.3 3.3 %collective-permute-start.5 = (bf16[3,64,448]{2,1,0:T(8,128)(2,1)S(1)}, bf16[3,64,448]{2,1,0:T(8,128)(2,1)S(1)}, u32[]{:S(2)}, u32[]{:S(2)}) collective-permute-start(bf16[3,64,448]{2,1,0:T(8,128)(2,1)S(1)} %get-tuple-element.16), channel_id=1, source_target_pairs={{1,0},{2,1},{3,2},{4,3},{5,4},{6,5},{7,6},{8,7},{9,8},{10,9},{11,1... | collective-permute-start | bytes 516104 | tf_op jit(solution)/shard_map/ppermute | solution.py:16
  41.3 10.8 %collective-permute-start.4 = (bf16[3,64,448]{2,1,0:T(8,128)(2,1)S(1)}, bf16[3,64,448]{2,1,0:T(8,128)(2,1)S(1)}, u32[]{:S(2)}, u32[]{:S(2)}) collective-permute-start(bf16[3,64,448]{2,1,0:T(8,128)(2,1)S(1)} %get-tuple-element.15), channel_id=1, source_target_pairs={{0,1},{1,2},{2,3},{3,4},{4,5},{5,6},{6,7},{7,8},{8,9},{9,10},{10,1... | collective-permute-start | bytes 516104 | tf_op jit(solution)/shard_map/ppermute | solution.py:14
  53.6 1.1 %copy-start.5 = (bf16[9,64,448]{2,1,0:T(8,128)(2,1)S(1)}, bf16[9,64,448]{2,1,0:T(8,128)(2,1)}, u32[]{:S(2)}) copy-start(bf16[9,64,448]{2,1,0:T(8,128)(2,1)} %param.6) | copy-start | bytes 1548292
  55.6 3.3 %collective-permute-start.7 = (bf16[3,64,448]{2,1,0:T(8,128)(2,1)S(1)}, bf16[3,64,448]{2,1,0:T(8,128)(2,1)S(1)}, u32[]{:S(2)}, u32[]{:S(2)}) collective-permute-start(bf16[3,64,448]{2,1,0:T(8,128)(2,1)S(1)} %get-tuple-element.14), channel_id=1, source_target_pairs={{1,0},{2,1},{3,2},{4,3},{5,4},{6,5},{7,6},{8,7},{9,8},{10,9},{11,1... | collective-permute-start | bytes 516104 | tf_op jit(solution)/shard_map/ppermute | solution.py:16
  55.7 10.6 %collective-permute-start.6 = (bf16[3,64,448]{2,1,0:T(8,128)(2,1)S(1)}, bf16[3,64,448]{2,1,0:T(8,128)(2,1)S(1)}, u32[]{:S(2)}, u32[]{:S(2)}) collective-permute-start(bf16[3,64,448]{2,1,0:T(8,128)(2,1)S(1)} %get-tuple-element.13), channel_id=1, source_target_pairs={{0,1},{1,2},{2,3},{3,4},{4,5},{5,6},{6,7},{7,8},{8,9},{9,10},{10,1... | collective-permute-start | bytes 516104 | tf_op jit(solution)/shard_map/ppermute | solution.py:14
  80.7 3.4 %copy-start.4 = (f32[9,448]{1,0:T(8,128)S(1)}, f32[9,448]{1,0:T(8,128)}, u32[]{:S(2)}) copy-start(f32[9,448]{1,0:T(8,128)} %copy-done.3) | copy-start | bytes 48388
where the time goes:
time: 86.8 us; the launch traced here: 86.3 us
  local copies, waits for them, and re-layouts  30.6 us (35%)
  waiting for transfers between devices  28 us (32%)
  starting transfers between devices  16.8 us (19%)
  other arithmetic  5.79 us (7%)
  matrix products  4.12 us (5%)
  between operations  1.05 us (1%)
    ppermute x4, waiting for transfers between devices, padded_2(): lax.ppermute(tail, axis, [(i, (i + 1) % count) for i in range(count)])  25 us
    ppermute x4, starting transfers between devices, padded_2(): lax.ppermute(head, axis, [((i + 1) % count, i) for i in range(count)])  15.7 us
    unnamed x37, local copies, waits for them, and re-layouts  9.54 us
    transpose x7, local copies, waits for them, and re-layouts, shards(): pieces.append(jnp.transpose(source, (0, 2, 1)))  5 us
    dot_general x4, matrix products, truncated(): jnp.einsum('irk,ikn->irn', left_matrix, panels, preferred_element_type=jn...  4.12 us
    slice x1, local copies, waits for them, and re-layouts, shards(): source = hls_four[offset:offset + row_count, :, 2 * reach_len - offset, :]  3.37 us
    convert_element_type x2, local copies, waits for them, and re-layouts, shards(): mirrored.astype(jnp.float32)  3.37 us
    concatenate x3, other arithmetic, padded_2(): jnp.concatenate([lax.ppermute(tail, axis, [(i, (i + 1) % count) for i in...  3.08 us
  transfers between devices with their start and end apart: 8, of which 7 were waited for; matrix products, arithmetic and copies ran while one was open for 4% of the time, Pallas kernels for 0%

commit v1 on v0

v1 whole, which is shorter than its diff:
```python
import jax
import jax.numpy as jnp
from jax import lax
from jax.experimental import pallas as pl
from jax.experimental.pallas import tpu as pltpu
from jax.sharding import PartitionSpec as P

BLK = 64
SLOTS = 7
REACH = 3
ROWS = 9
LANES = 512
AXES = ("dom", "col")


def shift_of(q):
    return 1 - q % 2


def column_of(q, position):
    return q - REACH + position - shift_of(q)


def halo_plan(side):
    if side == 0:
        rows = {"l": range(-3, 0), "s": range(-6, 0), "h": range(-3, 0)}
    else:
        rows = {"l": range(9, 12), "s": range(9, 15), "h": range(9, 12)}
    full, low, high = [], [], []
    for name in ("s", "l", "h"):
        for q in rows[name]:
            for chunk in range(4):
                need = []
                for position in (2 * chunk, 2 * chunk + 1):
                    slot = position - shift_of(q)
                    column = column_of(q, position)
                    inside = 0 <= slot < SLOTS
                    if name != "l":
                        inside = inside and (column >= -3 if side == 0 else column <= 11)
                    need.append(inside)
                a, b = (name, q, 2 * chunk), (name, q, 2 * chunk + 1)
                if all(need):
                    full.append((a, b))
                elif need[0]:
                    low.append(a)
                elif need[1]:
                    high.append(b)
    while low and high:
        full.append((low.pop(), high.pop()))
    rest = low + high
    while rest:
        a = rest.pop()
        full.append((a, rest.pop() if rest else None))
    return full


PLANS = (halo_plan(0), halo_plan(1))
CHUNKS = len(PLANS[0])


def pack_kernel(cross, l_hbm, s_hbm, h_hbm, out_ref, l_buf, s_buf, h_buf, sems):
    core = lax.rem(lax.axis_index("col"), 2)
    right = core if cross else 1 - core
    copies = [
        pltpu.make_async_copy(s_hbm.at[pl.ds(3 * right, 6)], s_buf, sems.at[0]),
        pltpu.make_async_copy(l_hbm.at[pl.ds(6 * right, 3)], l_buf, sems.at[1]),
        pltpu.make_async_copy(h_hbm.at[pl.ds(6 * right, 3)], h_buf, sems.at[2]),
    ]
    for copy in copies:
        copy.start()
    for copy in copies:
        copy.wait()
    bufs = {"l": l_buf, "s": s_buf, "h": h_buf}

    def write(side):
        def block(name, q, position):
            slot = position - shift_of(q)
            row = q - 9 if side == 1 else (q + 6 if name == "s" else q + 3)
            return bufs[name], row, slot

        for n, (a, b) in enumerate(PLANS[side]):
            ref, row, slot = block(*a)
            if b is not None and a[:2] == b[:2] and b[2] == a[2] + 1:
                chunk = ref[row, :, slot * BLK : (slot + 2) * BLK]
            else:
                first = ref[row, :, slot * BLK : (slot + 1) * BLK]
                if b is None:
                    second = jnp.zeros_like(first)
                else:
                    ref, row, slot = block(*b)
                    second = ref[row, :, slot * BLK : (slot + 1) * BLK]
                chunk = jnp.concatenate([first, second], axis=1)
            out_ref[n * BLK : (n + 1) * BLK, :] = chunk

    pl.when(right == 1)(lambda: write(0))
    pl.when(right == 0)(lambda: write(1))


def pack(cross, l_values, s_values, h_values):
    return pl.pallas_call(
        lambda *refs: pack_kernel(cross, *refs),
        out_shape=jax.ShapeDtypeStruct((CHUNKS * BLK, 128), jnp.bfloat16),
        in_specs=[pl.BlockSpec(memory_space=pl.ANY)] * 3,
        out_specs=pl.BlockSpec(memory_space=pltpu.VMEM),
        scratch_shapes=[
            pltpu.VMEM((3, BLK, SLOTS * BLK), jnp.bfloat16),
            pltpu.VMEM((6, BLK, SLOTS * BLK), jnp.bfloat16),
            pltpu.VMEM((3, BLK, SLOTS * BLK), jnp.bfloat16),
            pltpu.SemaphoreType.DMA((3,)),
        ],
        name="pack_cross" if cross else "pack_chip",
    )(l_values, s_values, h_values)


RANGE = {"s": (-6, 16), "l": (-4, 13), "h": (-3, 13), "p": (-4, 13), "g": (-4, 14), "t": (-1, 9)}
MASK_FIRST = -6
OFFSET = (-2, -1, -1, 0, 0, 1, 1, 2)


def rows_of(name, q, count=1):
    first = (q - RANGE[name][0]) * BLK
    return slice(first, first + count * BLK)


def compute_kernel(
    l_ref, s_ref, h_ref, cross_ref, chip_ref, mask_ref, kernel_ref, gradient_ref, *scratch
):
    st = dict(zip(("s", "l", "h", "p", "g", "t"), scratch))
    core = lax.rem(lax.axis_index("col"), 2)
    zero_chunk = jnp.zeros((BLK, 128), jnp.bfloat16)

    def mask_row(q, first, last):
        row = q - MASK_FIRST
        return mask_ref[row : row + 1, first * 128 : last * 128]

    def zero_row(name, q):
        st[name][rows_of(name, q), :] = jnp.zeros((BLK, LANES), jnp.bfloat16)

    for name, q in (("s", 15), ("l", -4), ("l", 12), ("h", 12), ("p", -4), ("g", -4), ("g", 13)):
        zero_row(name, q)

    for name, ref in (("s", s_ref), ("l", l_ref), ("h", h_ref)):
        for q in range(ROWS):
            values = ref[q]
            pad = jnp.zeros((BLK, BLK), jnp.bfloat16)
            parts = [pad, values] if shift_of(q) else [values, pad]
            stored = jnp.concatenate(parts, axis=1)
            st[name][rows_of(name, q), :] = stored * mask_row(q, 0, 4).astype(jnp.bfloat16)

    def unpack(side, ref):
        content = {}
        for n, (a, b) in enumerate(PLANS[side]):
            for half, key in ((0, a), (1, b)):
                if key is not None:
                    content[key] = (n, half)
        halo = {"s": range(-6, 0), "l": range(-3, 0), "h": range(-3, 0)}
        if side == 1:
            halo = {"s": range(9, 15), "l": range(9, 12), "h": range(9, 12)}
        for name in halo:
            for q in halo[name]:
                for chunk in range(4):
                    places = [content.get((name, q, 2 * chunk + half)) for half in (0, 1)]
                    if places == [None, None]:
                        values = zero_chunk
                    else:
                        n, half = next(p for p in places if p is not None)
                        if places[0] is not None and places[1] == (n, 1) and places[0] == (n, 0):
                            values = ref[n * BLK : (n + 1) * BLK, :]
                        else:
                            parts = []
                            for place in places:
                                if place is None:
                                    parts.append(jnp.zeros((BLK, BLK), jnp.bfloat16))
                                else:
                                    n, half = place
                                    parts.append(
                                        ref[n * BLK : (n + 1) * BLK, half * BLK : (half + 1) * BLK]
                                    )
                            values = jnp.concatenate(parts, axis=1)
                        values = values * mask_row(q, chunk, chunk + 1).astype(jnp.bfloat16)
                    st[name][rows_of(name, q), chunk * 128 : (chunk + 1) * 128] = values

    @pl.when(core == 1)
    def _():
        unpack(0, chip_ref)
        unpack(1, cross_ref)

    @pl.when(core == 0)
    def _():
        unpack(0, cross_ref)
        unpack(1, chip_ref)

    def product(left, right, q, first, last, depth=(0, 8)):
        lhs = st[left][rows_of(left, q, 2), depth[0] * BLK : depth[1] * BLK]
        slabs = []
        for r in range(*depth):
            parts = []
            for chunk in range(first, last):
                source = chunk - OFFSET[r]
                if 0 <= source < 4:
                    rows = rows_of(right, q - REACH + r)
                    parts.append(st[right][rows, source * 128 : (source + 1) * 128])
                else:
                    parts.append(zero_chunk)
            slabs.append(jnp.concatenate(parts, axis=1))
        rhs = jnp.concatenate(slabs, axis=0)
        return jnp.dot(lhs, rhs, preferred_element_type=jnp.float32)

    def pair_mask(q, first, last):
        width = (last - first) * 128
        return jnp.concatenate(
            [jnp.broadcast_to(mask_row(q + k, first, last), (BLK, width)) for k in (0, 1)], axis=0
        )

    def store_product(target, left, right, q, pieces, depth=(0, 8)):
        for first, last in pieces:
            values = product(left, right, q, first, last, depth) * pair_mask(q, first, last)
            st[target][rows_of(target, q, 2), first * 128 : last * 128] = values.astype(
                jnp.bfloat16
            )

    halves = ((0, 2), (2, 4))
    for q in range(-3, 13, 2):
        pieces = halves
        if q == -3:
            pieces = ((1, 2), (2, 4))
        elif q == 9:
            pieces = ((0, 2), (2, 3))
        elif q == 11:
            pieces = ((0, 2),)
        store_product("p", "l", "s", q, pieces)
    for q, chunk in ((-3, 0), (9, 3), (11, 2), (11, 3)):
        st["p"][rows_of("p", q, 2), chunk * 128 : (chunk + 1) * 128] = jnp.zeros(
            (2 * BLK, 128), jnp.bfloat16
        )

    for q in range(-1, 9, 2):
        store_product("t", "p", "l", q, halves)
    for q in range(-1, 9, 2):
        values = []
        for first, last in halves:
            quintic = product("t", "p", q, first, last) * pair_mask(q, first, last)
            lsl = st["t"][rows_of("t", q, 2), first * 128 : last * 128].astype(jnp.float32)
            values.append((3.0 * lsl - 2.0 * quintic).astype(jnp.bfloat16))
        values = jnp.concatenate(values, axis=1)
        if q >= 0:
            kernel_ref[q] = values[:BLK, : SLOTS * BLK]
        kernel_ref[q + 1] = values[BLK:, BLK:]

    store_product("g", "h", "p", -3, ((3, 4),), (2, 8))
    for q in range(-1, 9, 2):
        store_product("g", "h", "p", q, halves)
    store_product("g", "h", "p", 9, ((0, 2),), (0, 6))
    store_product("g", "h", "p", 11, ((0, 1),), (0, 4))

    def stored_chunk(q, chunk):
        return st["g"][rows_of("g", q), chunk * 128 : (chunk + 1) * 128].astype(jnp.float32)

    for pair in range(5):
        mirrored = {}
        for step in range(-2, 3):
            upper = zero_chunk.astype(jnp.float32)
            lower = upper
            if step >= -1:
                upper = stored_chunk(2 * (pair + step), 2 - step)
            if step <= 1:
                lower = stored_chunk(2 * (pair + step) + 1, 1 - step)
            mirrored[step] = jnp.transpose(jnp.concatenate([upper, lower], axis=0))
        for k in (0, 1):
            q = 2 * pair + k
            if q >= ROWS:
                continue
            chunks = []
            for chunk in range(4):
                other = mirrored[chunk - 2 + k][k * BLK : (k + 1) * BLK]
                summed = (stored_chunk(q, chunk) + other) * mask_row(q, chunk, chunk + 1)
                chunks.append(summed.astype(jnp.bfloat16))
            values = jnp.concatenate(chunks, axis=1)
            gradient_ref[q] = values[:, : SLOTS * BLK] if k else values[:, BLK:]


def compute(l_values, s_values, h_values, cross, chip, mask):
    vmem = pl.BlockSpec(memory_space=pltpu.VMEM)
    out = jax.ShapeDtypeStruct(l_values.shape, jnp.bfloat16)
    return pl.pallas_call(
        compute_kernel,
        out_shape=(out, out),
        in_specs=[vmem] * 6,
        out_specs=(vmem, vmem),
        scratch_shapes=[
            pltpu.VMEM(((RANGE[name][1] - RANGE[name][0]) * BLK, LANES), jnp.bfloat16)
            for name in ("s", "l", "h", "p", "g", "t")
        ],
        compiler_params=pltpu.CompilerParams(vmem_limit_bytes=48 * 1024 * 1024),
        name="compute",
    )(l_values, s_values, h_values, cross, chip, mask)


def local_mask(pattern):
    device = lax.axis_index(AXES)
    turned = pattern.T
    around = jnp.concatenate([turned[:, -6:], turned, turned[:, :7]], axis=1)
    near = lax.dynamic_slice(around, (0, device * ROWS), (SLOTS, 22)).T.astype(jnp.float32)
    even = jnp.pad(near, ((0, 0), (1, 0)))
    odd = jnp.pad(near, ((0, 0), (0, 1)))
    stored = jnp.where(jnp.arange(22)[:, None] % 2 == 0, even, odd)
    return jnp.broadcast_to(stored[:, :, None], (22, 8, BLK)).reshape(22, LANES)


def shards(l_values, s_values, h_values, pattern):
    count = lax.axis_size(AXES)
    cross_pairs, chip_pairs = [], []
    for i in range(0, count, 2):
        j = (i - 1) % count
        cross_pairs += [(i, j), (j, i)]
        chip_pairs += [(i, i + 1), (i + 1, i)]
    cross = lax.ppermute(pack(True, l_values, s_values, h_values), AXES, cross_pairs)
    chip = lax.ppermute(pack(False, l_values, s_values, h_values), AXES, chip_pairs)
    mask = local_mask(pattern)
    return compute(l_values, s_values, h_values, cross, chip, mask)


def solution(mesh):
    rows = P(AXES, None, None)
    return jax.shard_map(
        shards,
        mesh=mesh,
        in_specs=(rows, rows, rows, P()),
        out_specs=(rows, rows),
        check_vma=False,
    )
```

time: 86.8 us -> 24.5 us (0.28)
  local copies, waits for them, and re-layouts: 30.6 us -> 0.44 us
  waiting for transfers between devices: 28 us -> 6 us
  Pallas kernels: 0 us -> 8.1 us
  starting transfers between devices: 16.8 us -> 9.02 us
  other arithmetic: 5.79 us -> 0.1 us
  matrix products: 4.12 us -> 0 us
    ppermute x8 -> x2, waiting for transfers between devices: 28 us -> 6 us  [the longest x1 6 us: shards(): lax.ppermute(pack(True, l_values, s_values, h_values), AXES, cross_pairs)]
    unnamed x37 -> x8, local copies, waits for them, and re-layouts: 9.54 us -> 0.03 us
    pallas_call x0 -> x3, Pallas kernels: none -> 8.1 us  [the longest x2 4.32 us: pack(): pl.pallas_call(lambda *refs: pack_kernel(cross, *refs), out_shape=jax.Sha...]
    ppermute x8 -> x2, starting transfers between devices: 16.8 us -> 9.02 us  [the longest x1 8.93 us: shards(): lax.ppermute(pack(True, l_values, s_values, h_values), AXES, cross_pairs)]
    transpose x7 -> x0, local copies, waits for them, and re-layouts: 5 us -> none  [shards(): pieces.append(jnp.transpose(source, (0, 2, 1)))]
    slice x9 -> x2, local copies, waits for them, and re-layouts: 4.55 us -> 0.07 us  [local_mask(): around = jnp.concatenate([turned[:, -6:], turned, turned[:, :7]], axis=1)]
    dot_general x4 -> x0, matrix products: 4.12 us -> none  [truncated(): jnp.einsum('irk,ikn->irn', left_matrix, panels, preferred_element_type=jn...]
    reshape x3 -> x1, local copies, waits for them, and re-layouts: 3.7 us -> 0.08 us  [local_mask(): return jnp.broadcast_to(stored[:, :, None], (22, 8, BLK)).reshape(22, LANES)]
  transfers between devices with their start and end apart: 8 -> 2, of which waited for: 7 -> 1; matrix products, arithmetic and copies ran while one was open for 4% -> 2% of each run, Pallas kernels for 0% -> 9%
where the time goes in v1:
time: 24.5 us; the launch traced here: 24.4 us
  starting transfers between devices  9.02 us (37%)
  Pallas kernels  8.1 us (33%)
  waiting for transfers between devices  6 us (24%)
  between operations  0.72 us (3%)
  local copies, waits for them, and re-layouts  0.44 us (2%)
    ppermute x1, starting transfers between devices, shards(): lax.ppermute(pack(True, l_values, s_values, h_values), AXES, cross_pairs)  8.93 us
    ppermute x1, waiting for transfers between devices, shards(): lax.ppermute(pack(True, l_values, s_values, h_values), AXES, cross_pairs)  6 us
    pallas_call x2, Pallas kernels, pack(): pl.pallas_call(lambda *refs: pack_kernel(cross, *refs), out_shape=jax.Sha...  4.32 us
    pallas_call x1, Pallas kernels, compute(): pl.pallas_call(compute_kernel, out_shape=(out, out), in_specs=[vmem] * 6,...  3.78 us
  transfers between devices with their start and end apart: 2, of which 1 were waited for; matrix products, arithmetic and copies ran while one was open for 2% of the time, Pallas kernels for 9%

profile of v1, /device:TPU:0, one launch (start us, length us, event | category | flops | bytes accessed | tf_op | source)
XLA Modules:
  0.0 24.4 jit_solution(2149556006652358775)
XLA Ops:
  0.6 2.1 %pack_chip.1 = bf16[1856,128]{1,0:T(8,128)(2,1)} custom-call(bf16[9,64,448]{2,1,0:T(8,128)(2,1)} %l_ref.1, bf16[9,64,448]{2,1,0:T(8,128)(2,1)} %s_ref.1, bf16[9,64,448]{2,1,0:T(8,128)(2,1)} %h_ref.1), custom_call_target="tpu_custom_call" | custom-call | tf_op jit(solution)/shard_map/pack_chip/pallas_call | solution.py:100
  2.7 0.0 copy-start.3
  2.8 0.1 collective-permute-start.1
  2.9 0.0 copy-start
  2.9 0.0 copy-start.1
  2.9 0.0 copy-start.2
  2.9 2.2 %pack_cross.1 = bf16[1856,128]{1,0:T(8,128)(2,1)} custom-call(bf16[9,64,448]{2,1,0:T(8,128)(2,1)} %l_ref.1, bf16[9,64,448]{2,1,0:T(8,128)(2,1)} %s_ref.1, bf16[9,64,448]{2,1,0:T(8,128)(2,1)} %h_ref.1), custom_call_target="tpu_custom_call" | custom-call | tf_op jit(solution)/shard_map/pack_cross/pallas_call | solution.py:100
  5.1 8.9 %collective-permute-start = (bf16[1856,128]{1,0:T(8,128)(2,1)}, bf16[1856,128]{1,0:T(8,128)(2,1)S(1)}, u32[]{:S(2)}, u32[]{:S(2)}) collective-permute-start(bf16[1856,128]{1,0:T(8,128)(2,1)} %pack_cross.1), channel_id=1, source_target_pairs={{0,255},{255,0},{2,1},{1,2},{4,3},{3,4},{6,5},{5,6},{8,7},{7,8},{1... | collective-permute-start | bytes 1425416 | tf_op jit(solution)/shard_map/ppermute | solution.py:317
  14.0 0.0 copy-done.3
  14.1 0.1 slice.8
  14.1 0.1 concatenate.3
  14.2 0.1 convert_bitcast_fusion
  14.3 0.1 copy.6
  14.4 0.1 broadcast_in_dim.16
  14.5 0.1 reshape.25.mask_ref
  14.6 0.0 collective-permute-done.1.chip_ref
  14.6 6.0 %collective-permute-done.cross_ref = bf16[1856,128]{1,0:T(8,128)(2,1)S(1)} collective-permute-done((bf16[1856,128]{1,0:T(8,128)(2,1)}, bf16[1856,128]{1,0:T(8,128)(2,1)S(1)}, u32[]{:S(2)}, u32[]{:S(2)}) %collective-permute-start) | collective-permute-done | bytes 475168 | tf_op jit(solution)/shard_map/ppermute | solution.py:317
  20.6 0.0 copy-done
  20.6 0.0 copy-done.1
  20.6 0.0 copy-done.2
  20.6 3.8 %compute.1 = (bf16[9,64,448]{2,1,0:T(8,128)(2,1)}, bf16[9,64,448]{2,1,0:T(8,128)(2,1)}) custom-call(bf16[9,64,448]{2,1,0:T(8,128)(2,1)S(1)} %copy-done, bf16[9,64,448]{2,1,0:T(8,128)(2,1)S(1)} %copy-done.1, bf16[9,64,448]{2,1,0:T(8,128)(2,1)S(1)} %copy-done.2, bf16[1856,128]{1,0:T(8,128)(2,1)S(1)} %collective-permute-done.cross_ref, ...), custom_call_target="tpu_custom_call" | custom-call | tf_op jit(solution)/shard_map/compute/pallas_call | solution.py:285
  (3 shorter events, 0.0 us)
Async XLA Ops:
  2.7 11.3 %copy-start.3 = (s32[2304,7]{0,1:T(8,128)S(1)}, s32[2304,7]{0,1:T(8,128)}, u32[]{:S(2)}) copy-start(s32[2304,7]{0,1:T(8,128)} %param.7) | copy-start | bytes 193540
  2.8 11.8 %collective-permute-start.1 = (bf16[1856,128]{1,0:T(8,128)(2,1)}, bf16[1856,128]{1,0:T(8,128)(2,1)S(1)}, u32[]{:S(2)}, u32[]{:S(2)}) collective-permute-start(bf16[1856,128]{1,0:T(8,128)(2,1)} %pack_chip.1), channel_id=1, source_target_pairs={{0,1},{1,0},{2,3},{3,2},{4,5},{5,4},{6,7},{7,6},{8,9},{9,8},{10,11... | collective-permute-start | bytes 1425416 | tf_op jit(solution)/shard_map/ppermute | solution.py:318
  2.9 17.7 %copy-start = (bf16[9,64,448]{2,1,0:T(8,128)(2,1)S(1)}, bf16[9,64,448]{2,1,0:T(8,128)(2,1)}, u32[]{:S(2)}) copy-start(bf16[9,64,448]{2,1,0:T(8,128)(2,1)} %l_ref.1) | copy-start | bytes 1548292
  2.9 17.7 %copy-start.1 = (bf16[9,64,448]{2,1,0:T(8,128)(2,1)S(1)}, bf16[9,64,448]{2,1,0:T(8,128)(2,1)}, u32[]{:S(2)}) copy-start(bf16[9,64,448]{2,1,0:T(8,128)(2,1)} %s_ref.1) | copy-start | bytes 1548292
  2.9 17.7 %copy-start.2 = (bf16[9,64,448]{2,1,0:T(8,128)(2,1)S(1)}, bf16[9,64,448]{2,1,0:T(8,128)(2,1)}, u32[]{:S(2)}) copy-start(bf16[9,64,448]{2,1,0:T(8,128)(2,1)} %h_ref.1) | copy-start | bytes 1548292
  5.1 15.5 %collective-permute-start = (bf16[1856,128]{1,0:T(8,128)(2,1)}, bf16[1856,128]{1,0:T(8,128)(2,1)S(1)}, u32[]{:S(2)}, u32[]{:S(2)}) collective-permute-start(bf16[1856,128]{1,0:T(8,128)(2,1)} %pack_cross.1), channel_id=1, source_target_pairs={{0,255},{255,0},{2,1},{1,2},{4,3},{3,4},{6,5},{5,6},{8,7},{7,8},{1... | collective-permute-start | bytes 1425416 | tf_op jit(solution)/shard_map/ppermute | solution.py:317

commit v2 on v1

v2 whole, which is shorter than its diff:
```python
import jax
import jax.numpy as jnp
from jax import lax
from jax.experimental import pallas as pl
from jax.experimental.pallas import tpu as pltpu
from jax.sharding import PartitionSpec as P

BLK = 64
SLOTS = 7
REACH = 3
ROWS = 9
LANES = 512
AXES = ("dom", "col")


def shift_of(q):
    return 1 - q % 2


def column_of(q, position):
    return q - REACH + position - shift_of(q)


def halo_plan(side):
    if side == 0:
        rows = {"l": range(-3, 0), "s": range(-6, 0), "h": range(-3, 0)}
    else:
        rows = {"l": range(9, 12), "s": range(9, 15), "h": range(9, 12)}
    full, low, high = [], [], []
    for name in ("s", "l", "h"):
        for q in rows[name]:
            for chunk in range(4):
                need = []
                for position in (2 * chunk, 2 * chunk + 1):
                    slot = position - shift_of(q)
                    column = column_of(q, position)
                    inside = 0 <= slot < SLOTS
                    if name != "l":
                        inside = inside and (column >= -3 if side == 0 else column <= 11)
                    need.append(inside)
                a, b = (name, q, 2 * chunk), (name, q, 2 * chunk + 1)
                if all(need):
                    full.append((a, b))
                elif need[0]:
                    low.append(a)
                elif need[1]:
                    high.append(b)
    while low and high:
        full.append((low.pop(), high.pop()))
    rest = low + high
    while rest:
        a = rest.pop()
        full.append((a, rest.pop() if rest else None))
    return full


PLANS = (halo_plan(0), halo_plan(1))
CHUNKS = len(PLANS[0])
MASK_FIRST, MASK_ROWS = -6, 22
CHIP_PARTS = (CHUNKS // 2, CHUNKS - CHUNKS // 2)


def write_halo(side, block, out_refs):
    chunks = []
    for a, b in PLANS[side]:
        ref, row, lane = block(*a)
        if b is not None and a[:2] == b[:2] and b[2] == a[2] + 1:
            chunks.append(ref[row, :, lane : lane + 2 * BLK])
            continue
        first = ref[row, :, lane : lane + BLK]
        second = jnp.zeros_like(first)
        if b is not None:
            ref, row, lane = block(*b)
            second = ref[row, :, lane : lane + BLK]
        chunks.append(jnp.concatenate([first, second], axis=1))
    for out_ref in out_refs:
        for n in range(out_ref.shape[0] // BLK):
            out_ref[n * BLK : (n + 1) * BLK, :] = chunks.pop(0)


def sender_block(refs, side, first):
    def block(name, q, position):
        row = q - ROWS if side == 1 else q + ROWS
        return refs[name], row - first[name], (position - shift_of(q)) * BLK

    return block


def pack_cross_kernel(l_hbm, s_hbm, h_hbm, out_ref, l_buf, s_buf, h_buf, sems):
    core = lax.rem(lax.axis_index("col"), 2)
    copies = [
        pltpu.make_async_copy(s_hbm.at[pl.ds(3 * core, 6)], s_buf, sems.at[0]),
        pltpu.make_async_copy(l_hbm.at[pl.ds(6 * core, 3)], l_buf, sems.at[1]),
        pltpu.make_async_copy(h_hbm.at[pl.ds(6 * core, 3)], h_buf, sems.at[2]),
    ]
    for copy in copies:
        copy.start()
    for copy in copies:
        copy.wait()
    bufs = {"l": l_buf, "s": s_buf, "h": h_buf}
    last = sender_block(bufs, 0, {"l": 6, "s": 3, "h": 6})
    first = sender_block(bufs, 1, {"l": 0, "s": 0, "h": 0})
    pl.when(core == 1)(lambda: write_halo(0, last, (out_ref,)))
    pl.when(core == 0)(lambda: write_halo(1, first, (out_ref,)))


def pack_cross(l_values, s_values, h_values):
    hbm = pl.BlockSpec(memory_space=pltpu.HBM)
    return pl.pallas_call(
        pack_cross_kernel,
        out_shape=pltpu.VMEM((CHUNKS * BLK, 128), jnp.bfloat16),
        in_specs=[hbm] * 3,
        out_specs=pl.BlockSpec(memory_space=pltpu.VMEM),
        scratch_shapes=[
            pltpu.VMEM((3, BLK, SLOTS * BLK), jnp.bfloat16),
            pltpu.VMEM((6, BLK, SLOTS * BLK), jnp.bfloat16),
            pltpu.VMEM((3, BLK, SLOTS * BLK), jnp.bfloat16),
            pltpu.SemaphoreType.DMA((3,)),
        ],
        cost_estimate=pl.CostEstimate(flops=1, bytes_accessed=1, transcendentals=0),
        name="pack_cross",
    )(l_values, s_values, h_values)


def write_mask(pattern_ref, mask_ref):
    count, total = mask_ref.shape[0], pattern_ref.shape[1]
    device = lax.axis_index("dom") * lax.axis_size("col") + lax.axis_index("col")
    first = device * ROWS + MASK_FIRST + total
    wanted = lax.rem(first + lax.broadcasted_iota(jnp.int32, (count, total), 0), total)
    index = lax.broadcasted_iota(jnp.int32, (count, total), 1)
    picked = (wanted == index).astype(jnp.float32).astype(jnp.bfloat16)
    pattern = pattern_ref[...].astype(jnp.float32).astype(jnp.bfloat16)
    near = lax.dot_general(
        picked, pattern, (((1,), (1,)), ((), ())), preferred_element_type=jnp.float32
    )
    even = lax.rem(lax.broadcasted_iota(jnp.int32, (count, 1), 0), 2) == 0
    zero = jnp.zeros((count, 1), jnp.float32)
    slots = [zero] + [near[:, s : s + 1] for s in range(SLOTS)] + [zero]
    places = [jnp.where(even, slots[p], slots[p + 1]) for p in range(8)]
    low = lax.broadcasted_iota(jnp.int32, (count, 128), 1) < BLK
    for chunk in range(4):
        mask_ref[:, chunk * 128 : (chunk + 1) * 128] = jnp.where(
            low, places[2 * chunk], places[2 * chunk + 1]
        )


def pack_chip_kernel(l_ref, s_ref, h_ref, pattern_ref, after_ref, *out_refs):
    del after_ref
    *out_refs, mask_ref = out_refs
    write_mask(pattern_ref, mask_ref)
    core = lax.rem(lax.axis_index("col"), 2)
    refs = {"l": l_ref, "s": s_ref, "h": h_ref}
    whole = {"l": 0, "s": 0, "h": 0}
    pl.when(core == 0)(lambda: write_halo(0, sender_block(refs, 0, whole), out_refs))
    pl.when(core == 1)(lambda: write_halo(1, sender_block(refs, 1, whole), out_refs))


def pack_chip(l_values, s_values, h_values, turned, after):
    vmem = pl.BlockSpec(memory_space=pltpu.VMEM)
    return pl.pallas_call(
        pack_chip_kernel,
        out_shape=tuple(pltpu.VMEM((n * BLK, 128), jnp.bfloat16) for n in CHIP_PARTS)
        + (pltpu.VMEM((MASK_ROWS, LANES), jnp.float32),),
        in_specs=[vmem] * 5,
        out_specs=(vmem,) * (len(CHIP_PARTS) + 1),
        compiler_params=pltpu.CompilerParams(vmem_limit_bytes=8 * 1024 * 1024),
        cost_estimate=pl.CostEstimate(flops=1, bytes_accessed=1, transcendentals=0),
        name="pack_chip",
    )(l_values, s_values, h_values, turned, after)


NAMES = ("s", "l", "h", "p", "t", "g")
RANGE = {"s": (-6, 16), "l": (-4, 13), "h": (-3, 13), "p": (-4, 13), "t": (-1, 9), "g": (-3, 13)}
OFFSET = (-2, -1, -1, 0, 0, 1, 1, 2)
HALVES = ((0, 2), (2, 4))
HALO = (
    {"s": range(-6, 0), "l": range(-3, 0), "h": range(-3, 0)},
    {"s": range(9, 15), "l": range(9, 12), "h": range(9, 12)},
)
ZERO_ROWS = ((("l", -4), ("p", -4)), (("s", 15), ("l", 12), ("h", 12)))
ZERO_CHUNKS = (((-3, 0),), ((9, 3), (11, 2), (11, 3)))
LATE = (
    {"p": (-3, -1, 1), "t": (-1, 1), "g": (-3, -1, 1, 3, 5)},
    {"p": (5, 7, 9, 11), "t": (5, 7), "g": (1, 3, 5, 7, 9, 11)},
)
EARLY = (
    {"p": (3, 5, 7, 9, 11), "t": (3, 5, 7), "g": (7, 9, 11)},
    {"p": (-3, -1, 1, 3), "t": (-1, 1, 3), "g": (-3, -1)},
)


def rows_of(name, q, count=1):
    first = (q - RANGE[name][0]) * BLK
    return slice(first, first + count * BLK)


def is_late(core, name, q):
    if name in ("s", "l", "h"):
        return q < 0 if core == 0 else q >= ROWS
    group = q if q % 2 else q - 1
    if name == "p" and group < -3:
        return core == 0
    return group in LATE[core][name]


class Stored:
    def __init__(self, core, early, late, mask_ref):
        self.core, self.early, self.late, self.mask_ref = core, early, late, mask_ref

    def ref(self, name, q):
        use_late = self.late is not None and is_late(self.core, name, q)
        return (self.late if use_late else self.early)[name]

    def get(self, name, q, first=0, last=4):
        return self.ref(name, q)[rows_of(name, q), first * 128 : last * 128]

    def put(self, name, q, values, first=0, last=4):
        self.ref(name, q)[rows_of(name, q), first * 128 : last * 128] = values

    def mask(self, q, first, last):
        row = q - MASK_FIRST
        return self.mask_ref[row : row + 1, first * 128 : last * 128]

    def pair_mask(self, q, first, last):
        shape = (BLK, (last - first) * 128)
        return jnp.concatenate(
            [jnp.broadcast_to(self.mask(q + k, first, last), shape) for k in (0, 1)], axis=0
        )

    def own_rows(self, refs):
        pad = jnp.zeros((BLK, BLK), jnp.bfloat16)
        for name, ref in refs.items():
            for q in range(ROWS):
                values = ref[q]
                parts = [pad, values] if shift_of(q) else [values, pad]
                stored = jnp.concatenate(parts, axis=1)
                self.put(name, q, stored * self.mask(q, 0, 4).astype(jnp.bfloat16))

    def unpack(self, side, refs):
        pad = jnp.zeros((BLK, BLK), jnp.bfloat16)
        content = {}
        for n, keys in enumerate(PLANS[side]):
            for half, key in enumerate(keys):
                if key is not None:
                    content[key] = (n, half)

        def piece(n, first, last):
            for ref in refs:
                if n < ref.shape[0] // BLK:
                    break
                n -= ref.shape[0] // BLK
            return ref[n * BLK : (n + 1) * BLK, first * BLK : last * BLK]

        for name, rows in HALO[side].items():
            for q in rows:
                for chunk in range(4):
                    a, b = (content.get((name, q, 2 * chunk + half)) for half in (0, 1))
                    if a is None and b is None:
                        values = jnp.zeros((BLK, 128), jnp.bfloat16)
                    else:
                        if a is not None and b is not None and a[0] == b[0]:
                            values = piece(a[0], 0, 2)
                        else:
                            values = jnp.concatenate(
                                [pad if p is None else piece(p[0], p[1], p[1] + 1) for p in (a, b)],
                                axis=1,
                            )
                        values = values * self.mask(q, chunk, chunk + 1).astype(jnp.bfloat16)
                    self.put(name, q, values, chunk, chunk + 1)
        for name, q in ZERO_ROWS[side]:
            self.put(name, q, jnp.zeros((BLK, LANES), jnp.bfloat16))
        for q, chunk in ZERO_CHUNKS[side]:
            for k in (0, 1):
                self.put("p", q + k, jnp.zeros((BLK, 128), jnp.bfloat16), chunk, chunk + 1)

    def product(self, left, right, q, first, last, depth=(0, 8)):
        lhs = jnp.concatenate([self.get(left, q + k) for k in (0, 1)], axis=0)
        lhs = lhs[:, depth[0] * BLK : depth[1] * BLK]
        slabs = []
        for r in range(*depth):
            parts = []
            for chunk in range(first, last):
                source = chunk - OFFSET[r]
                if 0 <= source < 4:
                    parts.append(self.get(right, q - REACH + r, source, source + 1))
                else:
                    parts.append(jnp.zeros((BLK, 128), jnp.bfloat16))
            slabs.append(jnp.concatenate(parts, axis=1))
        rhs = jnp.concatenate(slabs, axis=0)
        return jnp.dot(lhs, rhs, preferred_element_type=jnp.float32)

    def put_product(self, target, left, right, q, pieces=HALVES, depth=(0, 8)):
        for first, last in pieces:
            values = self.product(left, right, q, first, last, depth)
            values = (values * self.pair_mask(q, first, last)).astype(jnp.bfloat16)
            self.ref(target, q)[rows_of(target, q, 2), first * 128 : last * 128] = values

    def product_ls(self, q):
        pieces = {-3: ((1, 2), (2, 4)), 9: ((0, 2), (2, 3)), 11: ((0, 2),)}.get(q, HALVES)
        self.put_product("p", "l", "s", q, pieces)

    def lsl_term(self, q):
        self.put_product("t", "p", "l", q)

    def hls_term(self, q):
        pieces, depth = {
            -3: (((3, 4),), (2, 8)),
            9: (((0, 2),), (0, 6)),
            11: (((0, 1),), (0, 4)),
        }.get(q, (HALVES, (0, 8)))
        self.put_product("g", "h", "p", q, pieces, depth)

    def kernel_rows(self, q, out_ref):
        values = []
        for first, last in HALVES:
            quintic = self.product("t", "p", q, first, last) * self.pair_mask(q, first, last)
            lsl = self.ref("t", q)[rows_of("t", q, 2), first * 128 : last * 128]
            values.append((3.0 * lsl.astype(jnp.float32) - 2.0 * quintic).astype(jnp.bfloat16))
        values = jnp.concatenate(values, axis=1)
        if q >= 0:
            out_ref[q] = values[:BLK, : SLOTS * BLK]
        out_ref[q + 1] = values[BLK:, BLK:]

    def gradient_rows(self, pair, out_ref):
        rows = [2 * pair + k for k in (0, 1) if 2 * pair + k < ROWS]
        zero = jnp.zeros((BLK, 128), jnp.bfloat16)
        mirrored = {}
        for step in range(-2, 3 if len(rows) == 2 else 2):
            upper = lower = zero
            if step >= -1:
                upper = self.get("g", 2 * (pair + step), 2 - step, 3 - step)
            if step <= 1:
                lower = self.get("g", 2 * (pair + step) + 1, 1 - step, 2 - step)
            mirrored[step] = jnp.transpose(jnp.concatenate([upper, lower], axis=0))
        for k, q in enumerate(rows):
            chunks = []
            for chunk in range(4):
                other = mirrored[chunk - 2 + k][k * BLK : (k + 1) * BLK].astype(jnp.float32)
                own = self.get("g", q, chunk, chunk + 1).astype(jnp.float32)
                summed = (own + other) * self.mask(q, chunk, chunk + 1)
                chunks.append(summed.astype(jnp.bfloat16))
            values = jnp.concatenate(chunks, axis=1)
            out_ref[q] = values[:, : SLOTS * BLK] if k else values[:, BLK:]


def early_kernel(l_ref, s_ref, h_ref, chip_a_ref, chip_b_ref, mask_ref, *outs):
    core = lax.rem(lax.axis_index("col"), 2)
    early = dict(zip(NAMES, outs))

    def run(which):
        st = Stored(which, early, None, mask_ref)
        st.own_rows({"s": s_ref, "l": l_ref, "h": h_ref})
        st.unpack(1 - which, (chip_a_ref, chip_b_ref))
        for q in EARLY[which]["p"]:
            st.product_ls(q)
        for q in EARLY[which]["t"]:
            st.lsl_term(q)
        for q in EARLY[which]["g"]:
            st.hls_term(q)

    pl.when(core == 0)(lambda: run(0))
    pl.when(core == 1)(lambda: run(1))


def stored_types():
    return [
        pltpu.VMEM(((RANGE[name][1] - RANGE[name][0]) * BLK, LANES), jnp.bfloat16)
        for name in NAMES
    ]


def compute_early(l_values, s_values, h_values, chip, mask):
    vmem = pl.BlockSpec(memory_space=pltpu.VMEM)
    return pl.pallas_call(
        early_kernel,
        out_shape=tuple(stored_types()),
        in_specs=[vmem] * 6,
        out_specs=(vmem,) * len(NAMES),
        compiler_params=pltpu.CompilerParams(vmem_limit_bytes=16 * 1024 * 1024),
        cost_estimate=pl.CostEstimate(flops=1, bytes_accessed=1, transcendentals=0),
        name="early",
    )(l_values, s_values, h_values, *chip, mask)


def late_kernel(cross_ref, mask_ref, *refs):
    early = dict(zip(NAMES, refs[:6]))
    kernel_hbm, gradient_hbm = refs[6:8]
    late = dict(zip(NAMES, refs[8:14]))
    kernel_buf, gradient_buf, sems = refs[14:]
    core = lax.rem(lax.axis_index("col"), 2)

    def run(which):
        st = Stored(which, early, late, mask_ref)
        copies = []

        def send(buf, hbm, first, count):
            copy = pltpu.make_async_copy(
                buf.at[first : first + count], hbm.at[first : first + count], sems.at[len(copies)]
            )
            copy.start()
            copies.append(copy)

        def kernel_rows(q):
            st.kernel_rows(q, kernel_buf)
            first = max(q, 0)
            send(kernel_buf, kernel_hbm, first, q + 2 - first)

        def gradient_rows(pair):
            st.gradient_rows(pair, gradient_buf)
            send(gradient_buf, gradient_hbm, 2 * pair, min(2, ROWS - 2 * pair))

        kernel_rows(7 if which == 0 else -1)
        st.unpack(which, (cross_ref,))
        for q in LATE[which]["p"]:
            st.product_ls(q)
        for q in LATE[which]["g"]:
            st.hls_term(q)
        for q in LATE[which]["t"]:
            st.lsl_term(q)
        order = (-1, 1, 3, 5) if which == 0 else (7, 5, 3, 1)
        for pair in range(5):
            gradient_rows(pair)
            if pair < 4:
                kernel_rows(order[pair])
        for copy in copies:
            copy.wait()

    pl.when(core == 0)(lambda: run(0))
    pl.when(core == 1)(lambda: run(1))


def compute_late(cross, mask, early):
    vmem = pl.BlockSpec(memory_space=pltpu.VMEM)
    hbm = pl.BlockSpec(memory_space=pl.ANY)
    out = jax.ShapeDtypeStruct((ROWS, BLK, SLOTS * BLK), jnp.bfloat16)
    buf = pltpu.VMEM((ROWS, BLK, SLOTS * BLK), jnp.bfloat16)
    return pl.pallas_call(
        late_kernel,
        out_shape=(out, out),
        in_specs=[vmem] * (2 + len(NAMES)),
        out_specs=(hbm, hbm),
        scratch_shapes=stored_types() + [buf, buf, pltpu.SemaphoreType.DMA((10,))],
        compiler_params=pltpu.CompilerParams(vmem_limit_bytes=16 * 1024 * 1024),
        name="late",
    )(cross, mask, *early)


def shards(l_values, s_values, h_values, pattern):
    count = lax.axis_size(AXES)
    cross_pairs, chip_pairs = [], []
    for i in range(0, count, 2):
        j = (i - 1) % count
        cross_pairs += [(i, j), (j, i)]
        chip_pairs += [(i, i + 1), (i + 1, i)]
    cross_out = pack_cross(l_values, s_values, h_values)
    cross = lax.ppermute(cross_out, AXES, cross_pairs)
    *chip_out, mask = pack_chip(l_values, s_values, h_values, pattern.T, cross_out)
    chip = [lax.ppermute(part, AXES, chip_pairs) for part in chip_out]
    early = compute_early(l_values, s_values, h_values, chip, mask)
    return compute_late(cross, mask, early)


def solution(mesh):
    rows = P(AXES, None, None)
    return jax.shard_map(
        shards,
        mesh=mesh,
        in_specs=(rows, rows, rows, P()),
        out_specs=(rows, rows),
        check_vma=False,
    )
```

time: 24.5 us -> 19.2 us (0.78)
  Pallas kernels: 8.1 us -> 5.27 us
  waiting for transfers between devices: 6 us -> 4.17 us
  local copies, waits for them, and re-layouts: 0.44 us -> 0.02 us
    pallas_call x3 -> x4, Pallas kernels: 8.1 us -> 5.27 us  [the longest x1 2.28 us: compute_late(): pl.pallas_call(late_kernel, out_shape=(out, out), in_specs=[vmem] * (2 +...]
    ppermute x2 -> x3, waiting for transfers between devices: 6 us -> 4.17 us  [the longest x1 2.84 us: shards(): cross = lax.ppermute(cross_out, AXES, cross_pairs)]
    ppermute x2 -> x3, starting transfers between devices: 9.02 us -> 8.89 us  [the longest x1 8.3 us: shards(): cross = lax.ppermute(cross_out, AXES, cross_pairs)]
  transfers between devices with their start and end apart: 2 -> 3, of which waited for: 1 -> 2; matrix products, arithmetic and copies ran while one was open for 2% -> 0% of each run, Pallas kernels for 9% -> 8%
where the time goes in v2:
time: 19.2 us; the launch traced here: 19.1 us
  starting transfers between devices  8.89 us (46%)
  Pallas kernels  5.27 us (27%)
  waiting for transfers between devices  4.17 us (22%)
  between operations  0.7 us (4%)
    ppermute x1, starting transfers between devices, shards(): cross = lax.ppermute(cross_out, AXES, cross_pairs)  8.3 us
    ppermute x1, waiting for transfers between devices, shards(): cross = lax.ppermute(cross_out, AXES, cross_pairs)  2.84 us
    pallas_call x1, Pallas kernels, compute_late(): pl.pallas_call(late_kernel, out_shape=(out, out), in_specs=[vmem] * (2 +...  2.28 us
    pallas_call x1, Pallas kernels, pack_cross(): pl.pallas_call(pack_cross_kernel, out_shape=pltpu.VMEM((CHUNKS * BLK, 128...  1.46 us
    ppermute x2, waiting for transfers between devices, shards(): chip = [lax.ppermute(part, AXES, chip_pairs) for part in chip_out]  1.33 us
    pallas_call x1, Pallas kernels, compute_early(): pl.pallas_call(early_kernel, out_shape=tuple(stored_types()), in_specs=[v...  1.08 us
    ppermute x2, starting transfers between devices, shards(): chip = [lax.ppermute(part, AXES, chip_pairs) for part in chip_out]  0.59 us
    pallas_call x1, Pallas kernels, pack_chip(): pl.pallas_call(pack_chip_kernel, out_shape=tuple((pltpu.VMEM((n * BLK, 12...  0.46 us
  transfers between devices with their start and end apart: 3, of which 2 were waited for; matrix products, arithmetic and copies ran while one was open for 0% of the time, Pallas kernels for 8%

profile of v2, /device:TPU:0, one launch (start us, length us, event | category | flops | bytes accessed | tf_op | source)
XLA Modules:
  0.0 19.1 jit_solution(5828986697379223850)
XLA Ops:
  0.6 0.0 copy-start.2
  0.6 0.0 copy-start.1
  0.7 0.0 copy-start
  0.7 0.0 copy-start.3
  0.7 1.5 %pack_cross.1.after_ref = bf16[1856,128]{1,0:T(8,128)(2,1)S(1)} custom-call(bf16[9,64,448]{2,1,0:T(8,128)(2,1)} %l_ref.3, bf16[9,64,448]{2,1,0:T(8,128)(2,1)} %s_ref.3, bf16[9,64,448]{2,1,0:T(8,128)(2,1)} %h_ref.3), custom_call_target="tpu_custom_call" | custom-call | flops 1 | bytes 1 | tf_op jit(solution)/shard_map/pack_cross/pallas_call | solution.py:109
  2.1 8.3 %collective-permute-start = (bf16[1856,128]{1,0:T(8,128)(2,1)S(1)}, bf16[1856,128]{1,0:T(8,128)(2,1)S(1)}, u32[]{:S(2)}, u32[]{:S(2)}) collective-permute-start(bf16[1856,128]{1,0:T(8,128)(2,1)S(1)} %pack_cross.1.after_ref), channel_id=1, source_target_pairs={{0,255},{255,0},{2,1},{1,2},{4,3},{3,4},{6,5},{5,6},{8,7},{7,8},{1... | collective-permute-start | bytes 1425416 | tf_op jit(solution)/shard_map/ppermute | solution.py:456
  10.4 0.0 copy-done.2
  10.4 0.0 copy-done.1
  10.4 0.0 copy-done
  10.4 0.0 copy-done.3
  10.4 0.5 %pack_chip.1 = (bf16[896,128]{1,0:T(8,128)(2,1)S(1)}, bf16[960,128]{1,0:T(8,128)(2,1)S(1)}, f32[22,512]{1,0:T(8,128)S(1)}) custom-call(bf16[9,64,448]{2,1,0:T(8,128)(2,1)S(1)} %copy-done, bf16[9,64,448]{2,1,0:T(8,128)(2,1)S(1)} %copy-done.1, bf16[9,64,448]{2,1,0:T(8,128)(2,1)S(1)} %copy-done.2, s32[7,2304]{1,0:T(8,128)S(1)} %bitcast.1, ...), custom_call_target="tpu_custom_call" | custom-call | flops 1 | bytes 1 | tf_op jit(solution)/shard_map/pack_chip/pallas_call | solution.py:160
  10.9 0.1 collective-permute-start.2
  11.0 0.5 %collective-permute-start.1 = (bf16[896,128]{1,0:T(8,128)(2,1)S(1)}, bf16[896,128]{1,0:T(8,128)(2,1)S(1)}, u32[]{:S(2)}, u32[]{:S(2)}) collective-permute-start(bf16[896,128]{1,0:T(8,128)(2,1)S(1)} %get-tuple-element.12), channel_id=1, source_target_pairs={{0,1},{1,0},{2,3},{3,2},{4,5},{5,4},{6,7},{7,6},{8,9},{9,8},{10,11... | collective-permute-start | bytes 688136 | tf_op jit(solution)/shard_map/ppermute | solution.py:458
  11.5 1.3 %collective-permute-done.1.chip_a_ref = bf16[896,128]{1,0:T(8,128)(2,1)S(1)} collective-permute-done((bf16[896,128]{1,0:T(8,128)(2,1)S(1)}, bf16[896,128]{1,0:T(8,128)(2,1)S(1)}, u32[]{:S(2)}, u32[]{:S(2)}) %collective-permute-start.1) | collective-permute-done | bytes 229408 | tf_op jit(solution)/shard_map/ppermute | solution.py:458
  12.8 0.0 collective-permute-done.2.chip_b_ref
  12.8 1.1 %early.1 = (bf16[1408,512]{1,0:T(8,128)(2,1)S(1)}, bf16[1088,512]{1,0:T(8,128)(2,1)S(1)}, bf16[1024,512]{1,0:T(8,128)(2,1)S(1)}, bf16[1088,512]{1,0:T(8,128)(2,1...) custom-call(bf16[9,64,448]{2,1,0:T(8,128)(2,1)S(1)} %copy-done, bf16[9,64,448]{2,1,0:T(8,128)(2,1)S(1)} %copy-done.1, ...), custom_call_target="tpu_custom_call" | custom-call | flops 1 | bytes 1 | tf_op jit(solution)/shard_map/early/pallas_call | solution.py:374
  13.9 2.8 %collective-permute-done.cross_ref = bf16[1856,128]{1,0:T(8,128)(2,1)S(1)} collective-permute-done((bf16[1856,128]{1,0:T(8,128)(2,1)S(1)}, bf16[1856,128]{1,0:T(8,128)(2,1)S(1)}, u32[]{:S(2)}, u32[]{:S(2)}) %collective-permute-start) | collective-permute-done | bytes 475168 | tf_op jit(solution)/shard_map/ppermute | solution.py:456
  16.8 2.3 %late.1 = (bf16[9,64,448]{2,1,0:T(8,128)(2,1)}, bf16[9,64,448]{2,1,0:T(8,128)(2,1)}) custom-call(bf16[1856,128]{1,0:T(8,128)(2,1)S(1)} %collective-permute-done.cross_ref, f32[22,512]{1,0:T(8,128)S(1)} %get-tuple-element.11.mask_ref, bf16[1408,512]{1,0:T(8,128)(2,1)S(1)} %get-tuple-element.14.refs_0_, bf16[1088,512]{1,0:T(8,128)(2,1)S(1)} %get-tuple-element.15.refs_1_, ...), custom_call_target="tpu_custom_call" | custom-call | tf_op jit(solution)/shard_map/late/pallas_call | solution.py:437
Async XLA Ops:
  0.6 9.8 %copy-start.2 = (bf16[9,64,448]{2,1,0:T(8,128)(2,1)S(1)}, bf16[9,64,448]{2,1,0:T(8,128)(2,1)}, u32[]{:S(2)}) copy-start(bf16[9,64,448]{2,1,0:T(8,128)(2,1)} %h_ref.3) | copy-start | bytes 1548292
  0.6 9.8 %copy-start.1 = (bf16[9,64,448]{2,1,0:T(8,128)(2,1)S(1)}, bf16[9,64,448]{2,1,0:T(8,128)(2,1)}, u32[]{:S(2)}) copy-start(bf16[9,64,448]{2,1,0:T(8,128)(2,1)} %s_ref.3) | copy-start | bytes 1548292
  0.7 9.8 %copy-start = (bf16[9,64,448]{2,1,0:T(8,128)(2,1)S(1)}, bf16[9,64,448]{2,1,0:T(8,128)(2,1)}, u32[]{:S(2)}) copy-start(bf16[9,64,448]{2,1,0:T(8,128)(2,1)} %l_ref.3) | copy-start | bytes 1548292
  0.7 9.8 %copy-start.3 = (s32[2304,7]{0,1:T(8,128)S(1)}, s32[2304,7]{0,1:T(8,128)}, u32[]{:S(2)}) copy-start(s32[2304,7]{0,1:T(8,128)} %param.7) | copy-start | bytes 193540
  2.1 14.6 %collective-permute-start = (bf16[1856,128]{1,0:T(8,128)(2,1)S(1)}, bf16[1856,128]{1,0:T(8,128)(2,1)S(1)}, u32[]{:S(2)}, u32[]{:S(2)}) collective-permute-start(bf16[1856,128]{1,0:T(8,128)(2,1)S(1)} %pack_cross.1.after_ref), channel_id=1, source_target_pairs={{0,255},{255,0},{2,1},{1,2},{4,3},{3,4},{6,5},{5,6},{8,7},{7,8},{1... | collective-permute-start | bytes 1425416 | tf_op jit(solution)/shard_map/ppermute | solution.py:456
  10.9 1.9 %collective-permute-start.2 = (bf16[960,128]{1,0:T(8,128)(2,1)S(1)}, bf16[960,128]{1,0:T(8,128)(2,1)S(1)}, u32[]{:S(2)}, u32[]{:S(2)}) collective-permute-start(bf16[960,128]{1,0:T(8,128)(2,1)S(1)} %get-tuple-element.13), channel_id=1, source_target_pairs={{0,1},{1,0},{2,3},{3,2},{4,5},{5,4},{6,7},{7,6},{8,9},{9,8},{10,11... | collective-permute-start | bytes 737288 | tf_op jit(solution)/shard_map/ppermute | solution.py:458
  11.0 1.8 %collective-permute-start.1 = (bf16[896,128]{1,0:T(8,128)(2,1)S(1)}, bf16[896,128]{1,0:T(8,128)(2,1)S(1)}, u32[]{:S(2)}, u32[]{:S(2)}) collective-permute-start(bf16[896,128]{1,0:T(8,128)(2,1)S(1)} %get-tuple-element.12), channel_id=1, source_target_pairs={{0,1},{1,0},{2,3},{3,2},{4,5},{5,4},{6,7},{7,6},{8,9},{9,8},{10,11... | collective-permute-start | bytes 688136 | tf_op jit(solution)/shard_map/ppermute | solution.py:458

commit v3 on v2

v3 whole, which is shorter than its diff:
```python
import functools

import jax
import jax.numpy as jnp
from jax import lax
from jax.experimental import pallas as pl
from jax.experimental.pallas import tpu as pltpu
from jax.sharding import PartitionSpec as P

BLK = 64
SLOTS = 7
REACH = 3
ROWS = 9
LANES = 512
AXES = ("dom", "col")


def shift_of(q):
    return 1 - q % 2


def column_of(q, position):
    return q - REACH + position - shift_of(q)


def halo_plan(side):
    if side == 0:
        rows = {"l": range(-3, 0), "s": range(-6, 0), "h": range(-3, 0)}
    else:
        rows = {"l": range(9, 12), "s": range(9, 15), "h": range(9, 12)}
    full, low, high = [], [], []
    for name in ("s", "l", "h"):
        for q in rows[name]:
            for chunk in range(4):
                need = []
                for position in (2 * chunk, 2 * chunk + 1):
                    slot = position - shift_of(q)
                    column = column_of(q, position)
                    inside = 0 <= slot < SLOTS
                    if name != "l":
                        inside = inside and (column >= -3 if side == 0 else column <= 11)
                    need.append(inside)
                a, b = (name, q, 2 * chunk), (name, q, 2 * chunk + 1)
                if all(need):
                    full.append((a, b))
                elif need[0]:
                    low.append(a)
                elif need[1]:
                    high.append(b)
    while low and high:
        full.append((low.pop(), high.pop()))
    rest = low + high
    while rest:
        a = rest.pop()
        full.append((a, rest.pop() if rest else None))
    return full


PLANS = (halo_plan(0), halo_plan(1))
CHUNKS = len(PLANS[0])
PACKED = CHUNKS * BLK - BLK // 2
CHIP_PARTS = (CHUNKS // 2 * BLK, PACKED - CHUNKS // 2 * BLK)
MASK_FIRST, MASK_ROWS = -6, 22


def write_halo(side, block, out_refs):
    for n, (a, b) in enumerate(PLANS[side]):
        ref, row, lane = block(*a)
        if b is None:
            only = ref[row, :, lane : lane + BLK]
            chunk = jnp.concatenate([only[: BLK // 2], only[BLK // 2 :]], axis=1)
        elif a[:2] == b[:2] and b[2] == a[2] + 1:
            chunk = ref[row, :, lane : lane + 2 * BLK]
        else:
            first = ref[row, :, lane : lane + BLK]
            ref, row, lane = block(*b)
            second = ref[row, :, lane : lane + BLK]
            chunk = jnp.concatenate([first, second], axis=1)
        place = n * BLK
        for out_ref in out_refs:
            if place < out_ref.shape[0]:
                break
            place -= out_ref.shape[0]
        out_ref[place : place + chunk.shape[0], :] = chunk


def sender_block(refs, side, first):
    def block(name, q, position):
        row = q - ROWS if side == 1 else q + ROWS
        return refs[name], row - first[name], (position - shift_of(q)) * BLK

    return block


def pack_cross_kernel(l_hbm, s_hbm, h_hbm, out_ref, l_buf, s_buf, h_buf, sems):
    core = lax.rem(lax.axis_index("col"), 2)
    copies = [
        pltpu.make_async_copy(s_hbm.at[pl.ds(3 * core, 6)], s_buf, sems.at[0]),
        pltpu.make_async_copy(l_hbm.at[pl.ds(6 * core, 3)], l_buf, sems.at[1]),
        pltpu.make_async_copy(h_hbm.at[pl.ds(6 * core, 3)], h_buf, sems.at[2]),
    ]
    for copy in copies:
        copy.start()
    bufs = {"l": l_buf, "s": s_buf, "h": h_buf}
    last = sender_block(bufs, 0, {"l": 6, "s": 3, "h": 6})
    first = sender_block(bufs, 1, {"l": 0, "s": 0, "h": 0})
    for copy in copies:
        copy.wait()
    pl.when(core == 1)(lambda: write_halo(0, last, (out_ref,)))
    pl.when(core == 0)(lambda: write_halo(1, first, (out_ref,)))


def pack_cross(l_values, s_values, h_values):
    hbm = pl.BlockSpec(memory_space=pltpu.HBM)
    return pl.pallas_call(
        pack_cross_kernel,
        out_shape=pltpu.VMEM((PACKED, 128), jnp.bfloat16),
        in_specs=[hbm] * 3,
        out_specs=pl.BlockSpec(memory_space=pltpu.VMEM),
        scratch_shapes=[
            pltpu.VMEM((3, BLK, SLOTS * BLK), jnp.bfloat16),
            pltpu.VMEM((6, BLK, SLOTS * BLK), jnp.bfloat16),
            pltpu.VMEM((3, BLK, SLOTS * BLK), jnp.bfloat16),
            pltpu.SemaphoreType.DMA((3,)),
        ],
        cost_estimate=pl.CostEstimate(flops=1, bytes_accessed=1, transcendentals=0),
        name="pack_cross",
    )(l_values, s_values, h_values)


def write_mask(pattern_ref, mask_ref):
    count, total = mask_ref.shape[0], pattern_ref.shape[1]
    device = lax.axis_index("dom") * lax.axis_size("col") + lax.axis_index("col")
    first = device * ROWS + MASK_FIRST + total
    wanted = lax.rem(first + lax.broadcasted_iota(jnp.int32, (count, total), 0), total)
    index = lax.broadcasted_iota(jnp.int32, (count, total), 1)
    picked = (wanted == index).astype(jnp.float32).astype(jnp.bfloat16)
    pattern = pattern_ref[...].astype(jnp.float32).astype(jnp.bfloat16)
    near = lax.dot_general(
        picked, pattern, (((1,), (1,)), ((), ())), preferred_element_type=jnp.float32
    )
    even = lax.rem(lax.broadcasted_iota(jnp.int32, (count, 1), 0), 2) == 0
    zero = jnp.zeros((count, 1), jnp.float32)
    slots = [zero] + [near[:, s : s + 1] for s in range(SLOTS)] + [zero]
    places = [jnp.where(even, slots[p], slots[p + 1]) for p in range(8)]
    low = lax.broadcasted_iota(jnp.int32, (count, 128), 1) < BLK
    for chunk in range(4):
        mask_ref[:, chunk * 128 : (chunk + 1) * 128] = jnp.where(
            low, places[2 * chunk], places[2 * chunk + 1]
        )


def pack_chip_kernel(l_ref, s_ref, h_ref, after_ref, *out_refs):
    del after_ref
    core = lax.rem(lax.axis_index("col"), 2)
    refs = {"l": l_ref, "s": s_ref, "h": h_ref}
    whole = {"l": 0, "s": 0, "h": 0}
    pl.when(core == 0)(lambda: write_halo(0, sender_block(refs, 0, whole), out_refs))
    pl.when(core == 1)(lambda: write_halo(1, sender_block(refs, 1, whole), out_refs))


def pack_chip(l_values, s_values, h_values, after):
    vmem = pl.BlockSpec(memory_space=pltpu.VMEM)
    return pl.pallas_call(
        pack_chip_kernel,
        out_shape=tuple(pltpu.VMEM((n, 128), jnp.bfloat16) for n in CHIP_PARTS),
        in_specs=[vmem] * 4,
        out_specs=(vmem,) * len(CHIP_PARTS),
        compiler_params=pltpu.CompilerParams(vmem_limit_bytes=8 * 1024 * 1024),
        cost_estimate=pl.CostEstimate(flops=1, bytes_accessed=1, transcendentals=0),
        name="pack_chip",
    )(l_values, s_values, h_values, after)


NAMES = ("s", "l", "h", "p", "t", "g")
RANGE = {"s": (-6, 16), "l": (-4, 13), "h": (-3, 13), "p": (-4, 13), "t": (-1, 9), "g": (-3, 13)}
FACTORS = {"p": ("l", "s"), "t": ("p", "l"), "g": ("h", "p"), "k": ("t", "p")}
GROUPS = {"p": range(-3, 13, 2), "t": range(-1, 9, 2), "g": range(-3, 13, 2), "k": range(-1, 9, 2)}
OFFSET = (-2, -1, -1, 0, 0, 1, 1, 2)
HALVES = ((0, 2), (2, 4))
PIECES = {
    ("p", -3): ((1, 2), (2, 4)),
    ("p", 9): ((0, 2), (2, 3)),
    ("p", 11): ((0, 2),),
    ("g", -3): ((3, 4),),
    ("g", 9): ((0, 2),),
    ("g", 11): ((0, 1),),
}
DEPTH = {("g", -3): (1, 4), ("g", 9): (0, 3), ("g", 11): (0, 2)}
SINGLE = {("t", -1): (1,), ("k", -1): (1,)}
HALO = (
    {"s": range(-6, 0), "l": range(-3, 0), "h": range(-3, 0)},
    {"s": range(9, 15), "l": range(9, 12), "h": range(9, 12)},
)
ZERO_ROWS = ((("l", -4), ("p", -4)), (("s", 15), ("l", 12), ("h", 12)))
ZERO_CHUNKS = (((-3, 0),), ((9, 3), (11, 2), (11, 3)))


@functools.cache
def phase_of(core, name, q):
    if name in ("s", "l", "h") or q < -3:
        if 0 <= q < ROWS:
            return 0
        return 2 if (q < 0) == (core == 0) else 1
    group = q if q % 2 else q - 1
    left, right = FACTORS[name]
    first, last = DEPTH.get((name, group), (0, 4))
    rows = range(group - REACH + 2 * first, group - REACH + 2 * last)
    return max(
        [phase_of(core, left, group + k) for k in (0, 1)]
        + [phase_of(core, right, m) for m in rows]
    )


@functools.cache
def early_pairs(core, name, q):
    left, right = FACTORS[name]
    if phase_of(core, name, q) < 2 or max(phase_of(core, left, q + k) for k in (0, 1)) == 2:
        return None
    first, last = DEPTH.get((name, q), (0, 4))
    pairs = [
        a
        for a in range(first, last)
        if max(phase_of(core, right, q - REACH + 2 * a + k) for k in (0, 1)) < 2
    ]
    if not pairs or (pairs[0] != first and pairs[-1] != last - 1):
        return None
    return pairs[0], pairs[-1] + 1


def partials_of(core, names):
    return [(name, q) for name in names for q in GROUPS[name] if early_pairs(core, name, q)]


def rows_of(name, q, count=1):
    first = (q - RANGE[name][0]) * BLK
    return slice(first, first + count * BLK)


class Stored:
    def __init__(self, core, arrays, mask_ref, partial_refs):
        self.core, self.arrays, self.mask_ref = core, arrays, mask_ref
        self.partial_refs = dict(zip(("p", "gk"), partial_refs))
        self.phase = len(arrays) - 1

    def get(self, name, q, first=0, last=4):
        ref = self.arrays[phase_of(self.core, name, q)][name]
        return ref[rows_of(name, q), first * 128 : last * 128]

    def put(self, name, q, values, first=0, last=4, count=1):
        ref = self.arrays[self.phase][name]
        ref[rows_of(name, q, count), first * 128 : last * 128] = values

    def mask(self, q, first, last):
        row = q - MASK_FIRST
        return self.mask_ref[row : row + 1, first * 128 : last * 128].astype(jnp.bfloat16)

    def pair_mask(self, name, q, first, last):
        shape = (BLK, (last - first) * 128)
        return jnp.concatenate(
            [
                jnp.broadcast_to(self.mask(q + k, first, last), shape)
                for k in SINGLE.get((name, q), (0, 1))
            ],
            axis=0,
        )

    def own_rows(self, refs):
        pad = jnp.zeros((BLK, BLK), jnp.bfloat16)
        for name, ref in refs.items():
            for q in range(ROWS):
                values = ref[q]
                parts = [pad, values] if shift_of(q) else [values, pad]
                stored = jnp.concatenate(parts, axis=1)
                self.put(name, q, stored * self.mask(q, 0, 4))

    def unpack(self, side, refs):
        pad = jnp.zeros((BLK, BLK), jnp.bfloat16)
        content = {}
        for n, keys in enumerate(PLANS[side]):
            for half, key in enumerate(keys):
                if key is not None:
                    content[key] = (n, half)

        def piece(n, first, last):
            place = n * BLK
            for ref in refs:
                if place < ref.shape[0]:
                    break
                place -= ref.shape[0]
            if n == CHUNKS - 1:
                halves = ref[place : place + BLK // 2, :]
                return jnp.concatenate([halves[:, :BLK], halves[:, BLK:]], axis=0)
            return ref[place : place + BLK, first * BLK : last * BLK]

        for name, rows in HALO[side].items():
            for q in rows:
                for chunk in range(4):
                    a, b = (content.get((name, q, 2 * chunk + half)) for half in (0, 1))
                    if a is None and b is None:
                        values = jnp.zeros((BLK, 128), jnp.bfloat16)
                    else:
                        if a is not None and b is not None and a[0] == b[0]:
                            values = piece(a[0], 0, 2)
                        else:
                            values = jnp.concatenate(
                                [pad if p is None else piece(p[0], p[1], p[1] + 1) for p in (a, b)],
                                axis=1,
                            )
                        values = values * self.mask(q, chunk, chunk + 1)
                    self.put(name, q, values, chunk, chunk + 1)
        for name, q in ZERO_ROWS[side]:
            self.put(name, q, jnp.zeros((BLK, LANES), jnp.bfloat16))
        for q, chunk in ZERO_CHUNKS[side]:
            zero = jnp.zeros((2 * BLK, 128), jnp.bfloat16)
            self.put("p", q, zero, chunk, chunk + 1, 2)

    def product(self, name, q, first, last, pairs):
        left, right = FACTORS[name]
        used = SINGLE.get((name, q), (0, 1))
        lhs = jnp.concatenate([self.get(left, q + k, *pairs) for k in used], axis=0)
        slabs = []
        for r in range(2 * pairs[0], 2 * pairs[1]):
            parts = []
            for chunk in range(first, last):
                source = chunk - OFFSET[r]
                if 0 <= source < 4:
                    parts.append(self.get(right, q - REACH + r, source, source + 1))
                else:
                    parts.append(jnp.zeros((BLK, 128), jnp.bfloat16))
            slabs.append(jnp.concatenate(parts, axis=1))
        rhs = jnp.concatenate(slabs, axis=0)
        return jnp.dot(lhs, rhs, preferred_element_type=jnp.float32)

    def partial_at(self, name, q):
        names = "p" if name == "p" else "gk"
        place = partials_of(self.core, names).index((name, q)) * 2 * BLK
        return self.partial_refs[names], slice(place, place + 2 * BLK)

    def put_partials(self, names):
        for name, q in partials_of(self.core, names):
            ref, rows = self.partial_at(name, q)
            for first, last in PIECES.get((name, q), HALVES):
                values = self.product(name, q, first, last, early_pairs(self.core, name, q))
                ref[rows, first * 128 : last * 128] = values

    def group(self, name, q):
        pairs, early = DEPTH.get((name, q), (0, 4)), None
        if self.phase == 2:
            early = early_pairs(self.core, name, q)
        if early:
            pairs = (early[1], pairs[1]) if early[0] == pairs[0] else (pairs[0], early[0])
        for first, last in PIECES.get((name, q), HALVES):
            values = self.product(name, q, first, last, pairs)
            if early:
                ref, rows = self.partial_at(name, q)
                values += ref[rows, first * 128 : last * 128]
            yield first, last, values

    def put_group(self, name, q):
        for first, last, values in self.group(name, q):
            values = values.astype(jnp.bfloat16) * self.pair_mask(name, q, first, last)
            used = SINGLE.get((name, q), (0, 1))
            self.put(name, q + used[0], values, first, last, len(used))

    def put_groups(self, names):
        for name in names:
            for q in GROUPS[name]:
                if phase_of(self.core, name, q) == self.phase:
                    self.put_group(name, q)

    def kernel_rows(self, q, out_ref):
        values = []
        used = SINGLE.get(("k", q), (0, 1))
        for first, last, quintic in self.group("k", q):
            lsl = jnp.concatenate([self.get("t", q + k, first, last) for k in used], axis=0)
            halved = (quintic - 1.5 * lsl.astype(jnp.float32)).astype(jnp.bfloat16)
            values.append(halved * (-2.0 * self.pair_mask("k", q, first, last)))
        values = jnp.concatenate(values, axis=1)
        if len(used) == 2:
            out_ref[q] = values[:BLK, : SLOTS * BLK]
        out_ref[q + 1] = values[-BLK:, BLK:]

    def gradient_rows(self, pair, out_ref):
        rows = [2 * pair + k for k in (0, 1) if 2 * pair + k < ROWS]
        zero = jnp.zeros((BLK, 128), jnp.bfloat16)
        mirrored = {}
        for step in range(-2, 3 if len(rows) == 2 else 2):
            upper = lower = zero
            if step >= -1:
                upper = self.get("g", 2 * (pair + step), 2 - step, 3 - step)
            if step <= 1:
                lower = self.get("g", 2 * (pair + step) + 1, 1 - step, 2 - step)
            mirrored[step] = jnp.transpose(jnp.concatenate([upper, lower], axis=0))
        for k, q in enumerate(rows):
            chunks = []
            for chunk in range(4):
                other = mirrored[chunk - 2 + k][k * BLK : (k + 1) * BLK]
                own = self.get("g", q, chunk, chunk + 1)
                chunks.append((own + other) * self.mask(q, chunk, chunk + 1))
            values = jnp.concatenate(chunks, axis=1)
            out_ref[q] = values[:, : SLOTS * BLK] if k else values[:, BLK:]


def stored_types(names):
    return tuple(
        pltpu.VMEM(((RANGE[name][1] - RANGE[name][0]) * BLK, LANES), jnp.bfloat16)
        for name in names
    )


def on_core(run):
    core = lax.rem(lax.axis_index("col"), 2)
    pl.when(core == 0)(lambda: run(0))
    pl.when(core == 1)(lambda: run(1))


LATE_ROUNDS = (
    (
        ("p1", "p-1", "p-3", "g5", "g3", "G4", "t1", "g1", "G3", "t-1",),
        ("g-1", "G2", "k5",),
        ("g-3", "G1", "k3",),
        ("k1", "G0",),
        ("k-1",),
    ),
    (
        ("p5", "p7", "p9", "p11", "g1", "g3", "g5", "G0", "t5", "t7", "g7", "G1",),
        ("g9", "k1", "G2",),
        ("g11", "k3", "G3",),
        ("k5", "G4",),
        ("k7",),
    ),
)
OWN_NAMES = ("s", "l", "h", "p", "t")
ROWS_TYPE = pltpu.VMEM((ROWS, BLK, SLOTS * BLK), jnp.bfloat16)


def vmem_call(kernel, operands, out_shape, name):
    vmem = pl.BlockSpec(memory_space=pltpu.VMEM)
    return pl.pallas_call(
        kernel,
        out_shape=out_shape,
        in_specs=[vmem] * len(operands),
        out_specs=(vmem,) * len(out_shape),
        compiler_params=pltpu.CompilerParams(vmem_limit_bytes=8 * 1024 * 1024),
        cost_estimate=pl.CostEstimate(flops=1, bytes_accessed=1, transcendentals=0),
        name=name,
    )(*operands)


def partial_type(names):
    count = max(len(partials_of(core, names)) for core in (0, 1))
    return pltpu.VMEM((count * 2 * BLK, LANES), jnp.float32)


def own_kernel(l_ref, s_ref, h_ref, pattern_ref, *outs):
    *outs, partial_ref, mask_ref = outs
    write_mask(pattern_ref, mask_ref)

    def run(core):
        st = Stored(core, [dict(zip(OWN_NAMES, outs))], mask_ref, [partial_ref])
        st.own_rows({"s": s_ref, "l": l_ref, "h": h_ref})
        st.put_groups("pt")
        st.put_partials("p")

    on_core(run)


def compute_own(l_values, s_values, h_values, turned):
    operands = (l_values, s_values, h_values, turned)
    mask = pltpu.VMEM((MASK_ROWS, LANES), jnp.float32)
    out = (*stored_types(OWN_NAMES), partial_type("p"), mask)
    *own, mask = vmem_call(own_kernel, operands, out, "own")
    return own, mask


def early_kernel(chip_a_ref, chip_b_ref, mask_ref, *refs):
    own, own_partial_ref = dict(zip(OWN_NAMES, refs[:5])), refs[5]
    early = dict(zip(NAMES, refs[6:12]))
    partial_ref, kernel_buf = refs[12:]

    def run(core):
        st = Stored(core, [own, early], mask_ref, [own_partial_ref, partial_ref])
        st.unpack(1 - core, (chip_a_ref, chip_b_ref))
        st.put_groups("ptg")
        for q in GROUPS["k"]:
            if phase_of(core, "k", q) < 2:
                st.kernel_rows(q, kernel_buf)
        st.put_partials("gk")

    on_core(run)


def compute_early(chip, mask, own):
    out = (*stored_types(NAMES), partial_type("gk"), ROWS_TYPE)
    return vmem_call(early_kernel, (*chip, mask, *own), out, "early")


def late_kernel(cross_ref, mask_ref, *refs):
    own, own_partial_ref = dict(zip(OWN_NAMES, refs[:5])), refs[5]
    early = dict(zip(NAMES, refs[6:12]))
    partial_ref, early_buf, kernel_hbm, gradient_hbm = refs[12:16]
    late = dict(zip(NAMES, refs[16:22]))
    kernel_buf, gradient_buf, sems = refs[22:]

    def run(core):
        st = Stored(core, [own, early, late], mask_ref, [own_partial_ref, partial_ref])
        copies = []

        def send(buf, hbm, first, last):
            for row in range(first, last):
                copy = pltpu.make_async_copy(buf.at[row], hbm.at[row], sems.at[len(copies)])
                copy.start()
                copies.append(copy)

        for q in GROUPS["k"]:
            if phase_of(core, "k", q) < 2:
                send(early_buf, kernel_hbm, max(q, 0), q + 2)
        st.unpack(core, (cross_ref,))
        for steps in LATE_ROUNDS[core]:
            ready = []
            for step in steps:
                name, q = step[0], int(step[1:])
                if name == "G":
                    st.gradient_rows(q, gradient_buf)
                    ready.append((gradient_buf, gradient_hbm, 2 * q, min(2 * q + 2, ROWS)))
                elif name == "k":
                    st.kernel_rows(q, kernel_buf)
                    ready.append((kernel_buf, kernel_hbm, max(q, 0), q + 2))
                else:
                    st.put_group(name, q)
            for item in ready:
                send(*item)
        for copy in copies:
            copy.wait()

    on_core(run)


def compute_late(cross, mask, own, early):
    vmem = pl.BlockSpec(memory_space=pltpu.VMEM)
    hbm = pl.BlockSpec(memory_space=pl.ANY)
    out = jax.ShapeDtypeStruct((ROWS, BLK, SLOTS * BLK), jnp.bfloat16)
    operands = (cross, mask, *own, *early)
    return pl.pallas_call(
        late_kernel,
        out_shape=(out, out),
        in_specs=[vmem] * len(operands),
        out_specs=(hbm, hbm),
        scratch_shapes=[
            *stored_types(NAMES),
            ROWS_TYPE,
            ROWS_TYPE,
            pltpu.SemaphoreType.DMA((2 * ROWS,)),
        ],
        compiler_params=pltpu.CompilerParams(vmem_limit_bytes=16 * 1024 * 1024),
        name="late",
    )(*operands)


def shards(l_values, s_values, h_values, pattern):
    count = lax.axis_size(AXES)
    cross_pairs, chip_pairs = [], []
    for i in range(0, count, 2):
        j = (i - 1) % count
        cross_pairs += [(i, j), (j, i)]
        chip_pairs += [(i, i + 1), (i + 1, i)]
    cross_out = pack_cross(l_values, s_values, h_values)
    cross = lax.ppermute(cross_out, AXES, cross_pairs)
    chip_out = pack_chip(l_values, s_values, h_values, cross_out)
    chip = [lax.ppermute(part, AXES, chip_pairs) for part in chip_out]
    own, mask = compute_own(l_values, s_values, h_values, pattern.T)
    early = compute_early(chip, mask, own)
    return compute_late(cross, mask, own, early)


def solution(mesh):
    rows = P(AXES, None, None)
    return jax.shard_map(
        shards,
        mesh=mesh,
        in_specs=(rows, rows, rows, P()),
        out_specs=(rows, rows),
        check_vma=False,
    )
```

time: 19.2 us -> 18.9 us (0.984)
  waiting for transfers between devices: 4.17 us -> 3.52 us
  Pallas kernels: 5.27 us -> 5.69 us
    ppermute x2, waiting for transfers between devices: 1.33 us -> 0.41 us  [shards(): chip = [lax.ppermute(part, AXES, chip_pairs) for part in chip_out]]
    pallas_call x4 -> x5, Pallas kernels: 5.27 us -> 5.69 us  [the longest x1 2.14 us: compute_late(): pl.pallas_call(late_kernel, out_shape=(out, out), in_specs=[vmem] * len(o...]
    ppermute x1, waiting for transfers between devices: 2.84 us -> 3.11 us  [shards(): cross = lax.ppermute(cross_out, AXES, cross_pairs)]
  transfers between devices with their start and end apart: 3 -> 3, of which waited for: 2 -> 2; matrix products, arithmetic and copies ran while one was open for 0% -> 0% of each run, Pallas kernels for 8% -> 11%
where the time goes in v3:
time: 18.9 us; the launch traced here: 18.8 us
  starting transfers between devices  8.89 us (47%)
  Pallas kernels  5.69 us (30%)
  waiting for transfers between devices  3.52 us (19%)
  between operations  0.71 us (4%)
    ppermute x1, starting transfers between devices, shards(): cross = lax.ppermute(cross_out, AXES, cross_pairs)  8.3 us
    ppermute x1, waiting for transfers between devices, shards(): cross = lax.ppermute(cross_out, AXES, cross_pairs)  3.11 us
    pallas_call x1, Pallas kernels, compute_late(): pl.pallas_call(late_kernel, out_shape=(out, out), in_specs=[vmem] * len(o...  2.14 us
    pallas_call x2, Pallas kernels, vmem_call(): pl.pallas_call(kernel, out_shape=out_shape, in_specs=[vmem] * len(operand...  1.93 us
    pallas_call x1, Pallas kernels, pack_cross(): pl.pallas_call(pack_cross_kernel, out_shape=pltpu.VMEM((PACKED, 128), jnp...  1.45 us
    ppermute x2, starting transfers between devices, shards(): chip = [lax.ppermute(part, AXES, chip_pairs) for part in chip_out]  0.59 us
    ppermute x2, waiting for transfers between devices, shards(): chip = [lax.ppermute(part, AXES, chip_pairs) for part in chip_out]  0.41 us
  transfers between devices with their start and end apart: 3, of which 2 were waited for; matrix products, arithmetic and copies ran while one was open for 0% of the time, Pallas kernels for 11%

profile of v3, /device:TPU:0, one launch (start us, length us, event | category | flops | bytes accessed | tf_op | source)
XLA Modules:
  0.0 18.8 jit_solution(4187438232645643585)
XLA Ops:
  0.6 0.0 copy-start.2
  0.6 0.0 copy-start.1
  0.6 0.0 copy-start
  0.7 1.4 %pack_cross.1.after_ref = bf16[1824,128]{1,0:T(8,128)(2,1)S(1)} custom-call(bf16[9,64,448]{2,1,0:T(8,128)(2,1)} %l_ref.3, bf16[9,64,448]{2,1,0:T(8,128)(2,1)} %s_ref.3, bf16[9,64,448]{2,1,0:T(8,128)(2,1)} %h_ref.3), custom_call_target="tpu_custom_call" | custom-call | flops 1 | bytes 1 | tf_op jit(solution)/shard_map/pack_cross/pallas_call | solution.py:115
  2.1 0.0 copy-start.3
  2.1 8.3 %collective-permute-start = (bf16[1824,128]{1,0:T(8,128)(2,1)S(1)}, bf16[1824,128]{1,0:T(8,128)(2,1)S(1)}, u32[]{:S(2)}, u32[]{:S(2)}) collective-permute-start(bf16[1824,128]{1,0:T(8,128)(2,1)S(1)} %pack_cross.1.after_ref), channel_id=1, source_target_pairs={{0,255},{255,0},{2,1},{1,2},{4,3},{3,4},{6,5},{5,6},{8,7},{7,8},{1... | collective-permute-start | bytes 1400840 | tf_op jit(solution)/shard_map/ppermute | solution.py:569
  10.4 0.0 copy-done.2
  10.4 0.0 copy-done.1
  10.4 0.0 copy-done
  10.4 0.2 pack_chip.1
  10.6 0.1 collective-permute-start.2
  10.7 0.5 %collective-permute-start.1 = (bf16[896,128]{1,0:T(8,128)(2,1)S(1)}, bf16[896,128]{1,0:T(8,128)(2,1)S(1)}, u32[]{:S(2)}, u32[]{:S(2)}) collective-permute-start(bf16[896,128]{1,0:T(8,128)(2,1)S(1)} %get-tuple-element.26), channel_id=1, source_target_pairs={{0,1},{1,0},{2,3},{3,2},{4,5},{5,4},{6,7},{7,6},{8,9},{9,8},{10,11... | collective-permute-start | bytes 688136 | tf_op jit(solution)/shard_map/ppermute | solution.py:571
  11.2 0.0 copy-done.3
  11.2 0.9 %own.1 = (bf16[1408,512]{1,0:T(8,128)(2,1)S(1)}, bf16[1088,512]{1,0:T(8,128)(2,1)S(1)}, bf16[1024,512]{1,0:T(8,128)(2,1)S(1)}, bf16[1088,512]{1,0:T(8,128)(2,1)S...) custom-call(bf16[9,64,448]{2,1,0:T(8,128)(2,1)S(1)} %copy-done, ...), custom_call_target="tpu_custom_call" | custom-call | flops 1 | bytes 1 | tf_op jit(solution)/shard_map/own/pallas_call | solution.py:440
  12.1 0.4 %collective-permute-done.1.chip_a_ref = bf16[896,128]{1,0:T(8,128)(2,1)S(1)} collective-permute-done((bf16[896,128]{1,0:T(8,128)(2,1)S(1)}, bf16[896,128]{1,0:T(8,128)(2,1)S(1)}, u32[]{:S(2)}, u32[]{:S(2)}) %collective-permute-start.1) | collective-permute-done | bytes 229408 | tf_op jit(solution)/shard_map/ppermute | solution.py:571
  12.5 0.0 collective-permute-done.2.chip_b_ref
  12.5 1.0 %early.1 = (bf16[1408,512]{1,0:T(8,128)(2,1)S(1)}, bf16[1088,512]{1,0:T(8,128)(2,1)S(1)}, bf16[1024,512]{1,0:T(8,128)(2,1)S(1)}, bf16[1088,512]{1,0:T(8,128)(2,1...) custom-call(bf16[896,128]{1,0:T(8,128)(2,1)S(1)} %collective-permute, ...), custom_call_target="tpu_custom_call" | custom-call | flops 1 | bytes 1 | tf_op jit(solution)/shard_map/early/pallas_call | solution.py:440
  13.6 3.1 %collective-permute-done.cross_ref = bf16[1824,128]{1,0:T(8,128)(2,1)S(1)} collective-permute-done((bf16[1824,128]{1,0:T(8,128)(2,1)S(1)}, bf16[1824,128]{1,0:T(8,128)(2,1)S(1)}, u32[]{:S(2)}, u32[]{:S(2)}) %collective-permute-start) | collective-permute-done | bytes 466976 | tf_op jit(solution)/shard_map/ppermute | solution.py:569
  16.7 2.1 %late.1 = (bf16[9,64,448]{2,1,0:T(8,128)(2,1)}, bf16[9,64,448]{2,1,0:T(8,128)(2,1)}) custom-call(bf16[1824,128]{1,0:T(8,128)(2,1)S(1)} %collective-permute-done.cross_ref, f32[22,512]{1,0:T(8,128)S(1)} %get-tuple-element.19.mask_ref, bf16[1408,512]{1,0:T(8,128)(2,1)S(1)} %get-tuple-element.20.refs_0_, bf16[1088,512]{1,0:T(8,128)(2,1)S(1)} %get-tuple-element.21.refs_1_, ...), custom_call_target="tpu_custom_call" | custom-call | tf_op jit(solution)/shard_map/late/pallas_call | solution.py:545
Async XLA Ops:
  0.6 9.8 %copy-start.2 = (bf16[9,64,448]{2,1,0:T(8,128)(2,1)S(1)}, bf16[9,64,448]{2,1,0:T(8,128)(2,1)}, u32[]{:S(2)}) copy-start(bf16[9,64,448]{2,1,0:T(8,128)(2,1)} %h_ref.3) | copy-start | bytes 1548292
  0.6 9.8 %copy-start.1 = (bf16[9,64,448]{2,1,0:T(8,128)(2,1)S(1)}, bf16[9,64,448]{2,1,0:T(8,128)(2,1)}, u32[]{:S(2)}) copy-start(bf16[9,64,448]{2,1,0:T(8,128)(2,1)} %s_ref.3) | copy-start | bytes 1548292
  0.6 9.8 %copy-start = (bf16[9,64,448]{2,1,0:T(8,128)(2,1)S(1)}, bf16[9,64,448]{2,1,0:T(8,128)(2,1)}, u32[]{:S(2)}) copy-start(bf16[9,64,448]{2,1,0:T(8,128)(2,1)} %l_ref.3) | copy-start | bytes 1548292
  2.1 9.1 %copy-start.3 = (s32[2304,7]{0,1:T(8,128)S(1)}, s32[2304,7]{0,1:T(8,128)}, u32[]{:S(2)}) copy-start(s32[2304,7]{0,1:T(8,128)} %param.7) | copy-start | bytes 193540
  2.1 14.6 %collective-permute-start = (bf16[1824,128]{1,0:T(8,128)(2,1)S(1)}, bf16[1824,128]{1,0:T(8,128)(2,1)S(1)}, u32[]{:S(2)}, u32[]{:S(2)}) collective-permute-start(bf16[1824,128]{1,0:T(8,128)(2,1)S(1)} %pack_cross.1.after_ref), channel_id=1, source_target_pairs={{0,255},{255,0},{2,1},{1,2},{4,3},{3,4},{6,5},{5,6},{8,7},{7,8},{1... | collective-permute-start | bytes 1400840 | tf_op jit(solution)/shard_map/ppermute | solution.py:569
  10.6 1.9 %collective-permute-start.2 = (bf16[928,128]{1,0:T(8,128)(2,1)S(1)}, bf16[928,128]{1,0:T(8,128)(2,1)S(1)}, u32[]{:S(2)}, u32[]{:S(2)}) collective-permute-start(bf16[928,128]{1,0:T(8,128)(2,1)S(1)} %get-tuple-element.27), channel_id=1, source_target_pairs={{0,1},{1,0},{2,3},{3,2},{4,5},{5,4},{6,7},{7,6},{8,9},{9,8},{10,11... | collective-permute-start | bytes 712712 | tf_op jit(solution)/shard_map/ppermute | solution.py:571
  10.7 1.8 %collective-permute-start.1 = (bf16[896,128]{1,0:T(8,128)(2,1)S(1)}, bf16[896,128]{1,0:T(8,128)(2,1)S(1)}, u32[]{:S(2)}, u32[]{:S(2)}) collective-permute-start(bf16[896,128]{1,0:T(8,128)(2,1)S(1)} %get-tuple-element.26), channel_id=1, source_target_pairs={{0,1},{1,0},{2,3},{3,2},{4,5},{5,4},{6,7},{7,6},{8,9},{9,8},{10,11... | collective-permute-start | bytes 688136 | tf_op jit(solution)/shard_map/ppermute | solution.py:571

commit v4 on v3

--- a/solution.py
+++ b/solution.py
@@ -215,6 +215,8 @@
 @functools.cache
 def early_pairs(core, name, q):
     left, right = FACTORS[name]
+    if name == "g" and q in GROUPS["k"] and early_pairs(core, "k", q) is None:
+        return None
     if phase_of(core, name, q) < 2 or max(phase_of(core, left, q + k) for k in (0, 1)) == 2:
         return None
     first, last = DEPTH.get((name, q), (0, 4))
@@ -315,10 +317,8 @@
             zero = jnp.zeros((2 * BLK, 128), jnp.bfloat16)
             self.put("p", q, zero, chunk, chunk + 1, 2)
 
-    def product(self, name, q, first, last, pairs):
-        left, right = FACTORS[name]
-        used = SINGLE.get((name, q), (0, 1))
-        lhs = jnp.concatenate([self.get(left, q + k, *pairs) for k in used], axis=0)
+    def multiply(self, factors, right, q, first, last, pairs):
+        lhs = jnp.concatenate([self.get(name, row, *pairs) for name, row in factors], axis=0)
         slabs = []
         for r in range(2 * pairs[0], 2 * pairs[1]):
             parts = []
@@ -332,6 +332,13 @@
         rhs = jnp.concatenate(slabs, axis=0)
         return jnp.dot(lhs, rhs, preferred_element_type=jnp.float32)
 
+    def factors_of(self, name, q):
+        return [(FACTORS[name][0], q + k) for k in SINGLE.get((name, q), (0, 1))]
+
+    def product(self, name, q, first, last, pairs):
+        right = FACTORS[name][1]
+        return self.multiply(self.factors_of(name, q), right, q, first, last, pairs)
+
     def partial_at(self, name, q):
         names = "p" if name == "p" else "gk"
         place = partials_of(self.core, names).index((name, q)) * 2 * BLK
@@ -344,24 +351,49 @@
                 values = self.product(name, q, first, last, early_pairs(self.core, name, q))
                 ref[rows, first * 128 : last * 128] = values
 
-    def group(self, name, q):
+    def late_pairs(self, name, q):
         pairs, early = DEPTH.get((name, q), (0, 4)), None
         if self.phase == 2:
             early = early_pairs(self.core, name, q)
         if early:
             pairs = (early[1], pairs[1]) if early[0] == pairs[0] else (pairs[0], early[0])
+        return pairs, early is not None
+
+    def add_partial(self, name, q, first, last, values):
+        ref, rows = self.partial_at(name, q)
+        return values + ref[rows, first * 128 : last * 128]
+
+    def group(self, name, q):
+        pairs, partial = self.late_pairs(name, q)
         for first, last in PIECES.get((name, q), HALVES):
             values = self.product(name, q, first, last, pairs)
-            if early:
-                ref, rows = self.partial_at(name, q)
-                values += ref[rows, first * 128 : last * 128]
+            if partial:
+                values = self.add_partial(name, q, first, last, values)
             yield first, last, values
+
+    def put_piece(self, name, q, first, last, values):
+        values = values.astype(jnp.bfloat16) * self.pair_mask(name, q, first, last)
+        used = SINGLE.get((name, q), (0, 1))
+        self.put(name, q + used[0], values, first, last, len(used))
 
     def put_group(self, name, q):
         for first, last, values in self.group(name, q):
-            values = values.astype(jnp.bfloat16) * self.pair_mask(name, q, first, last)
-            used = SINGLE.get((name, q), (0, 1))
-            self.put(name, q + used[0], values, first, last, len(used))
+            self.put_piece(name, q, first, last, values)
+
+    def put_both(self, q, out_ref):
+        pairs, partial = self.late_pairs("g", q)
+        assert self.late_pairs("k", q) == (pairs, partial)
+        factors = self.factors_of("g", q) + self.factors_of("k", q)
+        pieces = []
+        for first, last in HALVES:
+            values = self.multiply(factors, "p", q, first, last, pairs)
+            hls, quintic = values[: 2 * BLK], values[2 * BLK :]
+            if partial:
+                hls = self.add_partial("g", q, first, last, hls)
+                quintic = self.add_partial("k", q, first, last, quintic)
+            self.put_piece("g", q, first, last, hls)
+            pieces.append((first, last, quintic))
+        self.kernel_rows(q, out_ref, pieces)
 
     def put_groups(self, names):
         for name in names:
@@ -369,10 +401,10 @@
                 if phase_of(self.core, name, q) == self.phase:
                     self.put_group(name, q)
 
-    def kernel_rows(self, q, out_ref):
+    def kernel_rows(self, q, out_ref, pieces):
         values = []
         used = SINGLE.get(("k", q), (0, 1))
-        for first, last, quintic in self.group("k", q):
+        for first, last, quintic in pieces:
             lsl = jnp.concatenate([self.get("t", q + k, first, last) for k in used], axis=0)
             halved = (quintic - 1.5 * lsl.astype(jnp.float32)).astype(jnp.bfloat16)
             values.append(halved * (-2.0 * self.pair_mask("k", q, first, last)))
@@ -417,18 +449,17 @@
 
 LATE_ROUNDS = (
     (
-        ("p1", "p-1", "p-3", "g5", "g3", "G4", "t1", "g1", "G3", "t-1",),
-        ("g-1", "G2", "k5",),
-        ("g-3", "G1", "k3",),
-        ("k1", "G0",),
-        ("k-1",),
+        ("p1", "p-1", "p-3", "b5", "b3", "G4", "t1", "t-1", "G3",),
+        ("b1", "G2",),
+        ("b-1", "G1",),
+        ("g-3", "G0",),
     ),
     (
-        ("p5", "p7", "p9", "p11", "g1", "g3", "g5", "G0", "t5", "t7", "g7", "G1",),
-        ("g9", "k1", "G2",),
-        ("g11", "k3", "G3",),
-        ("k5", "G4",),
-        ("k7",),
+        ("p5", "p7", "p9", "p11", "b1", "b3", "t5", "t7", "G0",),
+        ("b5", "G1",),
+        ("b7", "G2",),
+        ("g9", "G3",),
+        ("g11", "G4",),
     ),
 )
 OWN_NAMES = ("s", "l", "h", "p", "t")
@@ -485,7 +516,7 @@
         st.put_groups("ptg")
         for q in GROUPS["k"]:
             if phase_of(core, "k", q) < 2:
-                st.kernel_rows(q, kernel_buf)
+                st.kernel_rows(q, kernel_buf, st.group("k", q))
         st.put_partials("gk")
 
     on_core(run)
@@ -524,8 +555,8 @@
                 if name == "G":
                     st.gradient_rows(q, gradient_buf)
                     ready.append((gradient_buf, gradient_hbm, 2 * q, min(2 * q + 2, ROWS)))
-                elif name == "k":
-                    st.kernel_rows(q, kernel_buf)
+                elif name == "b":
+                    st.put_both(q, kernel_buf)
                     ready.append((kernel_buf, kernel_hbm, max(q, 0), q + 2))
                 else:
                     st.put_group(name, q)

time: 18.9 us -> 18.9 us (level)
  no operation moved by 1% of the time
where the time goes in v4:
time: 18.9 us; the launch traced here: 18.8 us
  starting transfers between devices  8.89 us (47%)
  Pallas kernels  5.61 us (30%)
  waiting for transfers between devices  3.55 us (19%)
  between operations  0.71 us (4%)
    ppermute x1, starting transfers between devices, shards(): cross = lax.ppermute(cross_out, AXES, cross_pairs)  8.3 us
    ppermute x1, waiting for transfers between devices, shards(): cross = lax.ppermute(cross_out, AXES, cross_pairs)  3.14 us
    pallas_call x1, Pallas kernels, compute_late(): pl.pallas_call(late_kernel, out_shape=(out, out), in_specs=[vmem] * len(o...  2.09 us
    pallas_call x2, Pallas kernels, vmem_call(): pl.pallas_call(kernel, out_shape=out_shape, in_specs=[vmem] * len(operand...  1.9 us
    pallas_call x1, Pallas kernels, pack_cross(): pl.pallas_call(pack_cross_kernel, out_shape=pltpu.VMEM((PACKED, 128), jnp...  1.45 us
    ppermute x2, starting transfers between devices, shards(): chip = [lax.ppermute(part, AXES, chip_pairs) for part in chip_out]  0.59 us
    ppermute x2, waiting for transfers between devices, shards(): chip = [lax.ppermute(part, AXES, chip_pairs) for part in chip_out]  0.41 us
  transfers between devices with their start and end apart: 3, of which 2 were waited for; matrix products, arithmetic and copies ran while one was open for 0% of the time, Pallas kernels for 11%

profile of v4, /device:TPU:0, one launch (start us, length us, event | category | flops | bytes accessed | tf_op | source)
XLA Modules:
  0.0 18.8 jit_solution(11685556735266373643)
XLA Ops:
  0.6 0.0 copy-start.2
  0.6 0.0 copy-start.1
  0.6 0.0 copy-start
  0.7 1.4 %pack_cross.1.after_ref = bf16[1824,128]{1,0:T(8,128)(2,1)S(1)} custom-call(bf16[9,64,448]{2,1,0:T(8,128)(2,1)} %l_ref.3, bf16[9,64,448]{2,1,0:T(8,128)(2,1)} %s_ref.3, bf16[9,64,448]{2,1,0:T(8,128)(2,1)} %h_ref.3), custom_call_target="tpu_custom_call" | custom-call | flops 1 | bytes 1 | tf_op jit(solution)/shard_map/pack_cross/pallas_call | solution.py:115
  2.1 0.0 copy-start.3
  2.1 8.3 %collective-permute-start = (bf16[1824,128]{1,0:T(8,128)(2,1)S(1)}, bf16[1824,128]{1,0:T(8,128)(2,1)S(1)}, u32[]{:S(2)}, u32[]{:S(2)}) collective-permute-start(bf16[1824,128]{1,0:T(8,128)(2,1)S(1)} %pack_cross.1.after_ref), channel_id=1, source_target_pairs={{0,255},{255,0},{2,1},{1,2},{4,3},{3,4},{6,5},{5,6},{8,7},{7,8},{1... | collective-permute-start | bytes 1400840 | tf_op jit(solution)/shard_map/ppermute | solution.py:600
  10.4 0.0 copy-done.2
  10.4 0.0 copy-done.1
  10.4 0.0 copy-done
  10.4 0.2 pack_chip.1
  10.6 0.1 collective-permute-start.2
  10.7 0.5 %collective-permute-start.1 = (bf16[896,128]{1,0:T(8,128)(2,1)S(1)}, bf16[896,128]{1,0:T(8,128)(2,1)S(1)}, u32[]{:S(2)}, u32[]{:S(2)}) collective-permute-start(bf16[896,128]{1,0:T(8,128)(2,1)S(1)} %get-tuple-element.26), channel_id=1, source_target_pairs={{0,1},{1,0},{2,3},{3,2},{4,5},{5,4},{6,7},{7,6},{8,9},{9,8},{10,11... | collective-permute-start | bytes 688136 | tf_op jit(solution)/shard_map/ppermute | solution.py:602
  11.2 0.0 copy-done.3
  11.2 0.9 %own.1 = (bf16[1408,512]{1,0:T(8,128)(2,1)S(1)}, bf16[1088,512]{1,0:T(8,128)(2,1)S(1)}, bf16[1024,512]{1,0:T(8,128)(2,1)S(1)}, bf16[1088,512]{1,0:T(8,128)(2,1)S...) custom-call(bf16[9,64,448]{2,1,0:T(8,128)(2,1)S(1)} %copy-done, ...), custom_call_target="tpu_custom_call" | custom-call | flops 1 | bytes 1 | tf_op jit(solution)/shard_map/own/pallas_call | solution.py:471
  12.1 0.4 %collective-permute-done.1.chip_a_ref = bf16[896,128]{1,0:T(8,128)(2,1)S(1)} collective-permute-done((bf16[896,128]{1,0:T(8,128)(2,1)S(1)}, bf16[896,128]{1,0:T(8,128)(2,1)S(1)}, u32[]{:S(2)}, u32[]{:S(2)}) %collective-permute-start.1) | collective-permute-done | bytes 229408 | tf_op jit(solution)/shard_map/ppermute | solution.py:602
  12.5 0.0 collective-permute-done.2.chip_b_ref
  12.5 1.0 %early.1 = (bf16[1408,512]{1,0:T(8,128)(2,1)S(1)}, bf16[1088,512]{1,0:T(8,128)(2,1)S(1)}, bf16[1024,512]{1,0:T(8,128)(2,1)S(1)}, bf16[1088,512]{1,0:T(8,128)(2,1...) custom-call(bf16[896,128]{1,0:T(8,128)(2,1)S(1)} %collective-permute, ...), custom_call_target="tpu_custom_call" | custom-call | flops 1 | bytes 1 | tf_op jit(solution)/shard_map/early/pallas_call | solution.py:471
  13.5 3.1 %collective-permute-done.cross_ref = bf16[1824,128]{1,0:T(8,128)(2,1)S(1)} collective-permute-done((bf16[1824,128]{1,0:T(8,128)(2,1)S(1)}, bf16[1824,128]{1,0:T(8,128)(2,1)S(1)}, u32[]{:S(2)}, u32[]{:S(2)}) %collective-permute-start) | collective-permute-done | bytes 466976 | tf_op jit(solution)/shard_map/ppermute | solution.py:600
  16.7 2.1 %late.1 = (bf16[9,64,448]{2,1,0:T(8,128)(2,1)}, bf16[9,64,448]{2,1,0:T(8,128)(2,1)}) custom-call(bf16[1824,128]{1,0:T(8,128)(2,1)S(1)} %collective-permute-done.cross_ref, f32[22,512]{1,0:T(8,128)S(1)} %get-tuple-element.19.mask_ref, bf16[1408,512]{1,0:T(8,128)(2,1)S(1)} %get-tuple-element.20.refs_0_, bf16[1088,512]{1,0:T(8,128)(2,1)S(1)} %get-tuple-element.21.refs_1_, ...), custom_call_target="tpu_custom_call" | custom-call | tf_op jit(solution)/shard_map/late/pallas_call | solution.py:576
Async XLA Ops:
  0.6 9.8 %copy-start.2 = (bf16[9,64,448]{2,1,0:T(8,128)(2,1)S(1)}, bf16[9,64,448]{2,1,0:T(8,128)(2,1)}, u32[]{:S(2)}) copy-start(bf16[9,64,448]{2,1,0:T(8,128)(2,1)} %h_ref.3) | copy-start | bytes 1548292
  0.6 9.8 %copy-start.1 = (bf16[9,64,448]{2,1,0:T(8,128)(2,1)S(1)}, bf16[9,64,448]{2,1,0:T(8,128)(2,1)}, u32[]{:S(2)}) copy-start(bf16[9,64,448]{2,1,0:T(8,128)(2,1)} %s_ref.3) | copy-start | bytes 1548292
  0.6 9.8 %copy-start = (bf16[9,64,448]{2,1,0:T(8,128)(2,1)S(1)}, bf16[9,64,448]{2,1,0:T(8,128)(2,1)}, u32[]{:S(2)}) copy-start(bf16[9,64,448]{2,1,0:T(8,128)(2,1)} %l_ref.3) | copy-start | bytes 1548292
  2.1 9.1 %copy-start.3 = (s32[2304,7]{0,1:T(8,128)S(1)}, s32[2304,7]{0,1:T(8,128)}, u32[]{:S(2)}) copy-start(s32[2304,7]{0,1:T(8,128)} %param.7) | copy-start | bytes 193540
  2.1 14.6 %collective-permute-start = (bf16[1824,128]{1,0:T(8,128)(2,1)S(1)}, bf16[1824,128]{1,0:T(8,128)(2,1)S(1)}, u32[]{:S(2)}, u32[]{:S(2)}) collective-permute-start(bf16[1824,128]{1,0:T(8,128)(2,1)S(1)} %pack_cross.1.after_ref), channel_id=1, source_target_pairs={{0,255},{255,0},{2,1},{1,2},{4,3},{3,4},{6,5},{5,6},{8,7},{7,8},{1... | collective-permute-start | bytes 1400840 | tf_op jit(solution)/shard_map/ppermute | solution.py:600
  10.6 1.9 %collective-permute-start.2 = (bf16[928,128]{1,0:T(8,128)(2,1)S(1)}, bf16[928,128]{1,0:T(8,128)(2,1)S(1)}, u32[]{:S(2)}, u32[]{:S(2)}) collective-permute-start(bf16[928,128]{1,0:T(8,128)(2,1)S(1)} %get-tuple-element.27), channel_id=1, source_target_pairs={{0,1},{1,0},{2,3},{3,2},{4,5},{5,4},{6,7},{7,6},{8,9},{9,8},{10,11... | collective-permute-start | bytes 712712 | tf_op jit(solution)/shard_map/ppermute | solution.py:602
  10.7 1.8 %collective-permute-start.1 = (bf16[896,128]{1,0:T(8,128)(2,1)S(1)}, bf16[896,128]{1,0:T(8,128)(2,1)S(1)}, u32[]{:S(2)}, u32[]{:S(2)}) collective-permute-start(bf16[896,128]{1,0:T(8,128)(2,1)S(1)} %get-tuple-element.26), channel_id=1, source_target_pairs={{0,1},{1,0},{2,3},{3,2},{4,5},{5,4},{6,7},{7,6},{8,9},{9,8},{10,11... | collective-permute-start | bytes 688136 | tf_op jit(solution)/shard_map/ppermute | solution.py:602

commit v5 on v4

--- a/solution.py
+++ b/solution.py
@@ -345,11 +345,22 @@
         return self.partial_refs[names], slice(place, place + 2 * BLK)
 
     def put_partials(self, names):
-        for name, q in partials_of(self.core, names):
-            ref, rows = self.partial_at(name, q)
-            for first, last in PIECES.get((name, q), HALVES):
-                values = self.product(name, q, first, last, early_pairs(self.core, name, q))
-                ref[rows, first * 128 : last * 128] = values
+        todo = partials_of(self.core, names)
+        for name, q in todo:
+            pairs = early_pairs(self.core, name, q)
+            together = [name]
+            if name == "k":
+                continue
+            if name == "g" and ("k", q) in todo:
+                assert early_pairs(self.core, "k", q) == pairs
+                together.append("k")
+            factors = [factor for each in together for factor in self.factors_of(each, q)]
+            for first, last in HALVES:
+                values = self.multiply(factors, FACTORS[name][1], q, first, last, pairs)
+                for n, each in enumerate(together):
+                    ref, rows = self.partial_at(each, q)
+                    part = values[n * 2 * BLK : (n + 1) * 2 * BLK]
+                    ref[rows, first * 128 : last * 128] = part
 
     def late_pairs(self, name, q):
         pairs, early = DEPTH.get((name, q), (0, 4)), None
@@ -513,10 +524,13 @@
     def run(core):
         st = Stored(core, [own, early], mask_ref, [own_partial_ref, partial_ref])
         st.unpack(1 - core, (chip_a_ref, chip_b_ref))
-        st.put_groups("ptg")
-        for q in GROUPS["k"]:
-            if phase_of(core, "k", q) < 2:
-                st.kernel_rows(q, kernel_buf, st.group("k", q))
+        st.put_groups("pt")
+        both = [q for q in GROUPS["k"] if phase_of(core, "k", q) == 1]
+        for q in both:
+            st.put_both(q, kernel_buf)
+        for q in GROUPS["g"]:
+            if phase_of(core, "g", q) == 1 and q not in both:
+                st.put_group("g", q)
         st.put_partials("gk")
 
     on_core(run)

time: 18.9 us -> 18.9 us (level)
  no operation moved by 1% of the time
where the time goes in v5:
time: 18.9 us; the launch traced here: 18.8 us
  starting transfers between devices  8.89 us (47%)
  Pallas kernels  5.64 us (30%)
  waiting for transfers between devices  3.52 us (19%)
  between operations  0.71 us (4%)
    ppermute x1, starting transfers between devices, shards(): cross = lax.ppermute(cross_out, AXES, cross_pairs)  8.3 us
    ppermute x1, waiting for transfers between devices, shards(): cross = lax.ppermute(cross_out, AXES, cross_pairs)  3.11 us
    pallas_call x1, Pallas kernels, compute_late(): pl.pallas_call(late_kernel, out_shape=(out, out), in_specs=[vmem] * len(o...  2.09 us
    pallas_call x2, Pallas kernels, vmem_call(): pl.pallas_call(kernel, out_shape=out_shape, in_specs=[vmem] * len(operand...  1.93 us
    pallas_call x1, Pallas kernels, pack_cross(): pl.pallas_call(pack_cross_kernel, out_shape=pltpu.VMEM((PACKED, 128), jnp...  1.45 us
    ppermute x2, starting transfers between devices, shards(): chip = [lax.ppermute(part, AXES, chip_pairs) for part in chip_out]  0.59 us
    ppermute x2, waiting for transfers between devices, shards(): chip = [lax.ppermute(part, AXES, chip_pairs) for part in chip_out]  0.41 us
  transfers between devices with their start and end apart: 3, of which 2 were waited for; matrix products, arithmetic and copies ran while one was open for 0% of the time, Pallas kernels for 11%

profile of v5, /device:TPU:0, one launch (start us, length us, event | category | flops | bytes accessed | tf_op | source)
XLA Modules:
  0.0 18.8 jit_solution(11527588128116420353)
XLA Ops:
  0.6 0.0 copy-start.2
  0.6 0.0 copy-start.1
  0.6 0.0 copy-start
  0.7 1.4 %pack_cross.1.after_ref = bf16[1824,128]{1,0:T(8,128)(2,1)S(1)} custom-call(bf16[9,64,448]{2,1,0:T(8,128)(2,1)} %l_ref.3, bf16[9,64,448]{2,1,0:T(8,128)(2,1)} %s_ref.3, bf16[9,64,448]{2,1,0:T(8,128)(2,1)} %h_ref.3), custom_call_target="tpu_custom_call" | custom-call | flops 1 | bytes 1 | tf_op jit(solution)/shard_map/pack_cross/pallas_call | solution.py:115
  2.1 0.0 copy-start.3
  2.1 8.3 %collective-permute-start = (bf16[1824,128]{1,0:T(8,128)(2,1)S(1)}, bf16[1824,128]{1,0:T(8,128)(2,1)S(1)}, u32[]{:S(2)}, u32[]{:S(2)}) collective-permute-start(bf16[1824,128]{1,0:T(8,128)(2,1)S(1)} %pack_cross.1.after_ref), channel_id=1, source_target_pairs={{0,255},{255,0},{2,1},{1,2},{4,3},{3,4},{6,5},{5,6},{8,7},{7,8},{1... | collective-permute-start | bytes 1400840 | tf_op jit(solution)/shard_map/ppermute | solution.py:614
  10.4 0.0 copy-done.2
  10.4 0.0 copy-done.1
  10.4 0.0 copy-done
  10.4 0.2 pack_chip.1
  10.6 0.1 collective-permute-start.2
  10.7 0.5 %collective-permute-start.1 = (bf16[896,128]{1,0:T(8,128)(2,1)S(1)}, bf16[896,128]{1,0:T(8,128)(2,1)S(1)}, u32[]{:S(2)}, u32[]{:S(2)}) collective-permute-start(bf16[896,128]{1,0:T(8,128)(2,1)S(1)} %get-tuple-element.26), channel_id=1, source_target_pairs={{0,1},{1,0},{2,3},{3,2},{4,5},{5,4},{6,7},{7,6},{8,9},{9,8},{10,11... | collective-permute-start | bytes 688136 | tf_op jit(solution)/shard_map/ppermute | solution.py:616
  11.2 0.0 copy-done.3
  11.2 0.9 %own.1 = (bf16[1408,512]{1,0:T(8,128)(2,1)S(1)}, bf16[1088,512]{1,0:T(8,128)(2,1)S(1)}, bf16[1024,512]{1,0:T(8,128)(2,1)S(1)}, bf16[1088,512]{1,0:T(8,128)(2,1)S...) custom-call(bf16[9,64,448]{2,1,0:T(8,128)(2,1)S(1)} %copy-done, ...), custom_call_target="tpu_custom_call" | custom-call | flops 1 | bytes 1 | tf_op jit(solution)/shard_map/own/pallas_call | solution.py:482
  12.1 0.4 %collective-permute-done.1.chip_a_ref = bf16[896,128]{1,0:T(8,128)(2,1)S(1)} collective-permute-done((bf16[896,128]{1,0:T(8,128)(2,1)S(1)}, bf16[896,128]{1,0:T(8,128)(2,1)S(1)}, u32[]{:S(2)}, u32[]{:S(2)}) %collective-permute-start.1) | collective-permute-done | bytes 229408 | tf_op jit(solution)/shard_map/ppermute | solution.py:616
  12.5 0.0 collective-permute-done.2.chip_b_ref
  12.5 1.0 %early.1 = (bf16[1408,512]{1,0:T(8,128)(2,1)S(1)}, bf16[1088,512]{1,0:T(8,128)(2,1)S(1)}, bf16[1024,512]{1,0:T(8,128)(2,1)S(1)}, bf16[1088,512]{1,0:T(8,128)(2,1...) custom-call(bf16[896,128]{1,0:T(8,128)(2,1)S(1)} %collective-permute, ...), custom_call_target="tpu_custom_call" | custom-call | flops 1 | bytes 1 | tf_op jit(solution)/shard_map/early/pallas_call | solution.py:482
  13.6 3.1 %collective-permute-done.cross_ref = bf16[1824,128]{1,0:T(8,128)(2,1)S(1)} collective-permute-done((bf16[1824,128]{1,0:T(8,128)(2,1)S(1)}, bf16[1824,128]{1,0:T(8,128)(2,1)S(1)}, u32[]{:S(2)}, u32[]{:S(2)}) %collective-permute-start) | collective-permute-done | bytes 466976 | tf_op jit(solution)/shard_map/ppermute | solution.py:614
  16.7 2.1 %late.1 = (bf16[9,64,448]{2,1,0:T(8,128)(2,1)}, bf16[9,64,448]{2,1,0:T(8,128)(2,1)}) custom-call(bf16[1824,128]{1,0:T(8,128)(2,1)S(1)} %collective-permute-done.cross_ref, f32[22,512]{1,0:T(8,128)S(1)} %get-tuple-element.19.mask_ref, bf16[1408,512]{1,0:T(8,128)(2,1)S(1)} %get-tuple-element.20.refs_0_, bf16[1088,512]{1,0:T(8,128)(2,1)S(1)} %get-tuple-element.21.refs_1_, ...), custom_call_target="tpu_custom_call" | custom-call | tf_op jit(solution)/shard_map/late/pallas_call | solution.py:590
Async XLA Ops:
  0.6 9.8 %copy-start.2 = (bf16[9,64,448]{2,1,0:T(8,128)(2,1)S(1)}, bf16[9,64,448]{2,1,0:T(8,128)(2,1)}, u32[]{:S(2)}) copy-start(bf16[9,64,448]{2,1,0:T(8,128)(2,1)} %h_ref.3) | copy-start | bytes 1548292
  0.6 9.8 %copy-start.1 = (bf16[9,64,448]{2,1,0:T(8,128)(2,1)S(1)}, bf16[9,64,448]{2,1,0:T(8,128)(2,1)}, u32[]{:S(2)}) copy-start(bf16[9,64,448]{2,1,0:T(8,128)(2,1)} %s_ref.3) | copy-start | bytes 1548292
  0.6 9.8 %copy-start = (bf16[9,64,448]{2,1,0:T(8,128)(2,1)S(1)}, bf16[9,64,448]{2,1,0:T(8,128)(2,1)}, u32[]{:S(2)}) copy-start(bf16[9,64,448]{2,1,0:T(8,128)(2,1)} %l_ref.3) | copy-start | bytes 1548292
  2.1 9.1 %copy-start.3 = (s32[2304,7]{0,1:T(8,128)S(1)}, s32[2304,7]{0,1:T(8,128)}, u32[]{:S(2)}) copy-start(s32[2304,7]{0,1:T(8,128)} %param.7) | copy-start | bytes 193540
  2.1 14.6 %collective-permute-start = (bf16[1824,128]{1,0:T(8,128)(2,1)S(1)}, bf16[1824,128]{1,0:T(8,128)(2,1)S(1)}, u32[]{:S(2)}, u32[]{:S(2)}) collective-permute-start(bf16[1824,128]{1,0:T(8,128)(2,1)S(1)} %pack_cross.1.after_ref), channel_id=1, source_target_pairs={{0,255},{255,0},{2,1},{1,2},{4,3},{3,4},{6,5},{5,6},{8,7},{7,8},{1... | collective-permute-start | bytes 1400840 | tf_op jit(solution)/shard_map/ppermute | solution.py:614
  10.6 1.9 %collective-permute-start.2 = (bf16[928,128]{1,0:T(8,128)(2,1)S(1)}, bf16[928,128]{1,0:T(8,128)(2,1)S(1)}, u32[]{:S(2)}, u32[]{:S(2)}) collective-permute-start(bf16[928,128]{1,0:T(8,128)(2,1)S(1)} %get-tuple-element.27), channel_id=1, source_target_pairs={{0,1},{1,0},{2,3},{3,2},{4,5},{5,4},{6,7},{7,6},{8,9},{9,8},{10,11... | collective-permute-start | bytes 712712 | tf_op jit(solution)/shard_map/ppermute | solution.py:616
  10.7 1.8 %collective-permute-start.1 = (bf16[896,128]{1,0:T(8,128)(2,1)S(1)}, bf16[896,128]{1,0:T(8,128)(2,1)S(1)}, u32[]{:S(2)}, u32[]{:S(2)}) collective-permute-start(bf16[896,128]{1,0:T(8,128)(2,1)S(1)} %get-tuple-element.26), channel_id=1, source_target_pairs={{0,1},{1,0},{2,3},{3,2},{4,5},{5,4},{6,7},{7,6},{8,9},{9,8},{10,11... | collective-permute-start | bytes 688136 | tf_op jit(solution)/shard_map/ppermute | solution.py:616

commit v6 on v4

--- a/solution.py
+++ b/solution.py
@@ -187,7 +187,7 @@
     ("g", 11): ((0, 1),),
 }
 DEPTH = {("g", -3): (1, 4), ("g", 9): (0, 3), ("g", 11): (0, 2)}
-SINGLE = {("t", -1): (1,), ("k", -1): (1,)}
+SINGLE = {("t", -1): (1,), ("k", -1): (1,), ("p", 11): (0,), ("g", 11): (0,)}
 HALO = (
     {"s": range(-6, 0), "l": range(-3, 0), "h": range(-3, 0)},
     {"s": range(9, 15), "l": range(9, 12), "h": range(9, 12)},

time: 18.9 us -> 18.9 us (level)
  no operation moved by 1% of the time
where the time goes in v6:
time: 18.9 us; the launch traced here: 18.8 us
  starting transfers between devices  8.89 us (47%)
  Pallas kernels  5.62 us (30%)
  waiting for transfers between devices  3.55 us (19%)
  between operations  0.71 us (4%)
    ppermute x1, starting transfers between devices, shards(): cross = lax.ppermute(cross_out, AXES, cross_pairs)  8.3 us
    ppermute x1, waiting for transfers between devices, shards(): cross = lax.ppermute(cross_out, AXES, cross_pairs)  3.14 us
    pallas_call x1, Pallas kernels, compute_late(): pl.pallas_call(late_kernel, out_shape=(out, out), in_specs=[vmem] * len(o...  2.09 us
    pallas_call x2, Pallas kernels, vmem_call(): pl.pallas_call(kernel, out_shape=out_shape, in_specs=[vmem] * len(operand...  1.9 us
    pallas_call x1, Pallas kernels, pack_cross(): pl.pallas_call(pack_cross_kernel, out_shape=pltpu.VMEM((PACKED, 128), jnp...  1.45 us
    ppermute x2, starting transfers between devices, shards(): chip = [lax.ppermute(part, AXES, chip_pairs) for part in chip_out]  0.59 us
    ppermute x2, waiting for transfers between devices, shards(): chip = [lax.ppermute(part, AXES, chip_pairs) for part in chip_out]  0.41 us
  transfers between devices with their start and end apart: 3, of which 2 were waited for; matrix products, arithmetic and copies ran while one was open for 0% of the time, Pallas kernels for 11%

profile of v6, /device:TPU:0, one launch (start us, length us, event | category | flops | bytes accessed | tf_op | source)
XLA Modules:
  0.0 18.8 jit_solution(6274980387130772647)
XLA Ops:
  0.6 0.0 copy-start.2
  0.6 0.0 copy-start.1
  0.6 0.0 copy-start
  0.7 1.4 %pack_cross.1.after_ref = bf16[1824,128]{1,0:T(8,128)(2,1)S(1)} custom-call(bf16[9,64,448]{2,1,0:T(8,128)(2,1)} %l_ref.3, bf16[9,64,448]{2,1,0:T(8,128)(2,1)} %s_ref.3, bf16[9,64,448]{2,1,0:T(8,128)(2,1)} %h_ref.3), custom_call_target="tpu_custom_call" | custom-call | flops 1 | bytes 1 | tf_op jit(solution)/shard_map/pack_cross/pallas_call | solution.py:115
  2.1 0.0 copy-start.3
  2.1 8.3 %collective-permute-start = (bf16[1824,128]{1,0:T(8,128)(2,1)S(1)}, bf16[1824,128]{1,0:T(8,128)(2,1)S(1)}, u32[]{:S(2)}, u32[]{:S(2)}) collective-permute-start(bf16[1824,128]{1,0:T(8,128)(2,1)S(1)} %pack_cross.1.after_ref), channel_id=1, source_target_pairs={{0,255},{255,0},{2,1},{1,2},{4,3},{3,4},{6,5},{5,6},{8,7},{7,8},{1... | collective-permute-start | bytes 1400840 | tf_op jit(solution)/shard_map/ppermute | solution.py:600
  10.4 0.0 copy-done.2
  10.4 0.0 copy-done.1
  10.4 0.0 copy-done
  10.4 0.2 pack_chip.1
  10.6 0.1 collective-permute-start.2
  10.7 0.5 %collective-permute-start.1 = (bf16[896,128]{1,0:T(8,128)(2,1)S(1)}, bf16[896,128]{1,0:T(8,128)(2,1)S(1)}, u32[]{:S(2)}, u32[]{:S(2)}) collective-permute-start(bf16[896,128]{1,0:T(8,128)(2,1)S(1)} %get-tuple-element.26), channel_id=1, source_target_pairs={{0,1},{1,0},{2,3},{3,2},{4,5},{5,4},{6,7},{7,6},{8,9},{9,8},{10,11... | collective-permute-start | bytes 688136 | tf_op jit(solution)/shard_map/ppermute | solution.py:602
  11.2 0.0 copy-done.3
  11.2 0.9 %own.1 = (bf16[1408,512]{1,0:T(8,128)(2,1)S(1)}, bf16[1088,512]{1,0:T(8,128)(2,1)S(1)}, bf16[1024,512]{1,0:T(8,128)(2,1)S(1)}, bf16[1088,512]{1,0:T(8,128)(2,1)S...) custom-call(bf16[9,64,448]{2,1,0:T(8,128)(2,1)S(1)} %copy-done, ...), custom_call_target="tpu_custom_call" | custom-call | flops 1 | bytes 1 | tf_op jit(solution)/shard_map/own/pallas_call | solution.py:471
  12.1 0.4 %collective-permute-done.1.chip_a_ref = bf16[896,128]{1,0:T(8,128)(2,1)S(1)} collective-permute-done((bf16[896,128]{1,0:T(8,128)(2,1)S(1)}, bf16[896,128]{1,0:T(8,128)(2,1)S(1)}, u32[]{:S(2)}, u32[]{:S(2)}) %collective-permute-start.1) | collective-permute-done | bytes 229408 | tf_op jit(solution)/shard_map/ppermute | solution.py:602
  12.5 0.0 collective-permute-done.2.chip_b_ref
  12.5 1.0 %early.1 = (bf16[1408,512]{1,0:T(8,128)(2,1)S(1)}, bf16[1088,512]{1,0:T(8,128)(2,1)S(1)}, bf16[1024,512]{1,0:T(8,128)(2,1)S(1)}, bf16[1088,512]{1,0:T(8,128)(2,1...) custom-call(bf16[896,128]{1,0:T(8,128)(2,1)S(1)} %collective-permute, ...), custom_call_target="tpu_custom_call" | custom-call | flops 1 | bytes 1 | tf_op jit(solution)/shard_map/early/pallas_call | solution.py:471
  13.5 3.1 %collective-permute-done.cross_ref = bf16[1824,128]{1,0:T(8,128)(2,1)S(1)} collective-permute-done((bf16[1824,128]{1,0:T(8,128)(2,1)S(1)}, bf16[1824,128]{1,0:T(8,128)(2,1)S(1)}, u32[]{:S(2)}, u32[]{:S(2)}) %collective-permute-start) | collective-permute-done | bytes 466976 | tf_op jit(solution)/shard_map/ppermute | solution.py:600
  16.7 2.1 %late.1 = (bf16[9,64,448]{2,1,0:T(8,128)(2,1)}, bf16[9,64,448]{2,1,0:T(8,128)(2,1)}) custom-call(bf16[1824,128]{1,0:T(8,128)(2,1)S(1)} %collective-permute-done.cross_ref, f32[22,512]{1,0:T(8,128)S(1)} %get-tuple-element.19.mask_ref, bf16[1408,512]{1,0:T(8,128)(2,1)S(1)} %get-tuple-element.20.refs_0_, bf16[1088,512]{1,0:T(8,128)(2,1)S(1)} %get-tuple-element.21.refs_1_, ...), custom_call_target="tpu_custom_call" | custom-call | tf_op jit(solution)/shard_map/late/pallas_call | solution.py:576
Async XLA Ops:
  0.6 9.8 %copy-start.2 = (bf16[9,64,448]{2,1,0:T(8,128)(2,1)S(1)}, bf16[9,64,448]{2,1,0:T(8,128)(2,1)}, u32[]{:S(2)}) copy-start(bf16[9,64,448]{2,1,0:T(8,128)(2,1)} %h_ref.3) | copy-start | bytes 1548292
  0.6 9.8 %copy-start.1 = (bf16[9,64,448]{2,1,0:T(8,128)(2,1)S(1)}, bf16[9,64,448]{2,1,0:T(8,128)(2,1)}, u32[]{:S(2)}) copy-start(bf16[9,64,448]{2,1,0:T(8,128)(2,1)} %s_ref.3) | copy-start | bytes 1548292
  0.6 9.8 %copy-start = (bf16[9,64,448]{2,1,0:T(8,128)(2,1)S(1)}, bf16[9,64,448]{2,1,0:T(8,128)(2,1)}, u32[]{:S(2)}) copy-start(bf16[9,64,448]{2,1,0:T(8,128)(2,1)} %l_ref.3) | copy-start | bytes 1548292
  2.1 9.1 %copy-start.3 = (s32[2304,7]{0,1:T(8,128)S(1)}, s32[2304,7]{0,1:T(8,128)}, u32[]{:S(2)}) copy-start(s32[2304,7]{0,1:T(8,128)} %param.7) | copy-start | bytes 193540
  2.1 14.6 %collective-permute-start = (bf16[1824,128]{1,0:T(8,128)(2,1)S(1)}, bf16[1824,128]{1,0:T(8,128)(2,1)S(1)}, u32[]{:S(2)}, u32[]{:S(2)}) collective-permute-start(bf16[1824,128]{1,0:T(8,128)(2,1)S(1)} %pack_cross.1.after_ref), channel_id=1, source_target_pairs={{0,255},{255,0},{2,1},{1,2},{4,3},{3,4},{6,5},{5,6},{8,7},{7,8},{1... | collective-permute-start | bytes 1400840 | tf_op jit(solution)/shard_map/ppermute | solution.py:600
  10.6 1.9 %collective-permute-start.2 = (bf16[928,128]{1,0:T(8,128)(2,1)S(1)}, bf16[928,128]{1,0:T(8,128)(2,1)S(1)}, u32[]{:S(2)}, u32[]{:S(2)}) collective-permute-start(bf16[928,128]{1,0:T(8,128)(2,1)S(1)} %get-tuple-element.27), channel_id=1, source_target_pairs={{0,1},{1,0},{2,3},{3,2},{4,5},{5,4},{6,7},{7,6},{8,9},{9,8},{10,11... | collective-permute-start | bytes 712712 | tf_op jit(solution)/shard_map/ppermute | solution.py:602
  10.7 1.8 %collective-permute-start.1 = (bf16[896,128]{1,0:T(8,128)(2,1)S(1)}, bf16[896,128]{1,0:T(8,128)(2,1)S(1)}, u32[]{:S(2)}, u32[]{:S(2)}) collective-permute-start(bf16[896,128]{1,0:T(8,128)(2,1)S(1)} %get-tuple-element.26), channel_id=1, source_target_pairs={{0,1},{1,0},{2,3},{3,2},{4,5},{5,4},{6,7},{7,6},{8,9},{9,8},{10,11... | collective-permute-start | bytes 688136 | tf_op jit(solution)/shard_map/ppermute | solution.py:602
